TPU v7x, 32 devices: a whole 2x2x4 slice. The times are simulated.
32 devices in a mesh: freq: 4 (over x, core), sky: 8 (over z, y).
Axes of the slice: x: 2, y: 2, z: 4, core: 2. Of those that a mesh axis runs over, the one named last changes fastest.
Arguments:
- sky_cube: bfloat16 [16, 256, 1024], P('freq', 'sky'), may hold values from -6 to 6
- half_width: int32 [16], P('freq'), may hold values from 2 to 12, as said below
- conv_weight: bfloat16 [16, 27], replicated, may hold values from -0.3125 to 0.3125
- out_cotangent: bfloat16 [16, 16, 256, 1024], P(None, 'freq', 'sky'), may hold values from -6 to 6
Outputs:
- sky_grad: float32 [16, 256, 1024], P('freq', 'sky')
- kernel_grad: float32 [16, 27], replicated
Inputs may be any that keep to these rules, and one draw needn't show every extreme that they name: half_width[f] differs by at most one from 2 + floor((10) (15 - f) / 15); the first frequency has exactly 12 and the last exactly 2.
All inputs are finite; a program needn't handle non-finite values.
Results may differ from a plain program's by a relative error of at most 0.0033.
Values may be sent and summed in bfloat16 or wider, within the bound.
A program may use at most 128 MiB of HBM per device.

v0:
```python
import math

import jax
import jax.numpy as jnp
from jax import lax
from jax.experimental import pallas as pl
from jax.experimental.pallas import tpu as pltpu
from jax.sharding import PartitionSpec as P

MAXH = 12
HALO = 16
PAD = 128
BLOCK = 128
EDGE = 40
BROWS = 48
F32 = jnp.float32
BF16 = jnp.bfloat16
MESH = pl.DeviceIdType.MESH
DIRS = [(df, ds) for df in (-1, 0, 1) for ds in (-1, 0, 1) if (df, ds) != (0, 0)]


def iota(shape, dim):
    return lax.broadcasted_iota(jnp.int32, shape, dim)


def row_of(r, rows):
    return jnp.where(r <= rows, r, jnp.where(r == rows + 1, -1, -1000))


def band_mask(b, height, rows, width):
    shape = (height, width)
    return row_of(iota(shape, 0), rows) == lax.rem(iota(shape, 1), rows) + (b - 1)


def shift_next(x):
    n = x.shape[-1]
    return jnp.where(iota(x.shape, 1) == n - 1, 0.0, pltpu.roll(x, n - 1, 1))


def shift_prev(x):
    n = x.shape[-1]
    return jnp.where(iota(x.shape, 1) == 0, 0.0, pltpu.roll(x, 1, 1))


def body(nf, ns, scale, hw_ref, sky_ref, w_ref, cot_ref, out_ref, kg_ref,
         skyh, gbh, cotv, bmat, acc, part, eu, ed, pf, pe, bs, tcol, trow, hwb,
         mine, slots, mine2, slots2,
         cot_sem, own_sem, s_sky, r_sky, s_hw, r_hw, s_part, r_part, s_gb, r_gb,
         s_kg, r_kg, s_kf, r_kf):
    planes, rows, length = out_ref.shape
    chans = w_ref.shape[0]
    wide = chans * rows
    tall = rows + 2 * HALO
    fi, si = lax.axis_index("freq"), lax.axis_index("sky")

    def valid(df, ds):
        ok = None
        for at, step, size in ((fi, df, nf), (si, ds, ns)):
            if step:
                one = at + step < size if step > 0 else at + step >= 0
                ok = one if ok is None else jnp.logical_and(ok, one)
        return ok

    def span(step, own_lo, own_n, halo_n, full_n):
        if step == 0:
            return own_lo, 0, own_n
        if step > 0:
            return own_lo - halo_n, own_n - halo_n, halo_n
        return own_lo + own_n, 0, halo_n

    lanes = pl.ds(PAD, length)

    cot_copies = [pltpu.make_async_copy(cot_ref.at[:, g], cotv.at[g], cot_sem.at[g])
                  for g in range(planes)]
    for copy in cot_copies:
        copy.start()
    own = pltpu.make_async_copy(
        sky_ref, skyh.at[pl.ds(1, planes), pl.ds(HALO, rows), lanes], own_sem.at[0])
    own.start()
    for ref in (skyh, gbh):
        n = ref.shape[0]
        ref[:, :, 0:PAD] = jnp.zeros((n, tall, PAD), BF16)
        ref[:, :, PAD + length:] = jnp.zeros((n, tall, PAD), BF16)
    for k in range(planes):
        hwb[1 + k] = jnp.full((8, 256), hw_ref[k].astype(F32))

    def dst_sky(df, ds):
        p0, _, pn = span(df, 1, planes, 1, planes + 2)
        r0, _, rn = span(ds, HALO, rows, HALO, tall)
        return skyh.at[pl.ds(p0, pn), pl.ds(r0, rn), lanes]

    for i, (df, ds) in enumerate(DIRS):
        @pl.when(jnp.logical_not(valid(-df, -ds)))
        def _(df=df, ds=ds):
            ref = dst_sky(df, ds)
            ref[...] = jnp.zeros(ref.shape, BF16)
            if df == 0:
                r0, _, rn = span(ds, HALO, rows, HALO, tall)
                gbh[:, r0:r0 + rn, PAD:PAD + length] = jnp.zeros((planes, rn, length), BF16)
            if ds == 0:
                hwb[0 if df > 0 else planes + 1] = jnp.ones((8, 256), F32)
                pf[0 if df > 0 else 1] = jnp.zeros((rows, length), F32)
            else:
                pe[(df + 1) * 2 + (ds > 0)] = jnp.zeros((8, length), F32)

    barrier = pltpu.get_barrier_semaphore()
    for k in range(1, ns):
        pl.semaphore_signal(barrier, inc=1, device_id=(fi, lax.rem(si + k, ns)), device_id_type=MESH)
    for k in range(1, nf):
        pl.semaphore_signal(barrier, inc=1, device_id=(lax.rem(fi + k, nf), si), device_id_type=MESH)
    greeted = jnp.int32(ns + nf - 2)
    for df, ds in DIRS:
        if df and ds:
            ok = valid(df, ds)
            greeted = greeted + jnp.where(ok, 1, 0)

            @pl.when(ok)
            def _(df=df, ds=ds):
                pl.semaphore_signal(barrier, inc=1, device_id=(fi + df, si + ds), device_id_type=MESH)

    pl.semaphore_wait(barrier, greeted)

    def remote(src, dst, send, recv, df, ds):
        return pltpu.make_async_remote_copy(
            src_ref=src, dst_ref=dst, send_sem=send, recv_sem=recv,
            device_id=(fi + df, si + ds), device_id_type=MESH)

    def sky_copy(i, df, ds):
        _, p0, pn = span(df, 1, planes, 1, planes + 2)
        _, r0, rn = span(ds, HALO, rows, HALO, tall)
        return remote(sky_ref.at[pl.ds(p0, pn), pl.ds(r0, rn), :], dst_sky(df, ds),
                      s_sky.at[i], r_sky.at[i], df, ds)

    def hw_copy(df):
        j = 0 if df > 0 else 1
        return remote(hwb.at[planes if df > 0 else 1], hwb.at[0 if df > 0 else planes + 1],
                      s_hw.at[j], r_hw.at[j], df, 0)

    def part_copy(i, df, ds):
        if ds == 0:
            src, dst = part.at[planes + 1 if df > 0 else 0, pl.ds(0, rows)], pf.at[0 if df > 0 else 1]
        else:
            src, dst = (ed if ds > 0 else eu), pe.at[(df + 1) * 2 + (ds > 0)]
        return remote(src, dst, s_part.at[i], r_part.at[i], df, ds)

    def gb_copy(ds):
        j = 0 if ds > 0 else 1
        r0, r1, rn = span(ds, HALO, rows, HALO, tall)
        return remote(gbh.at[:, pl.ds(HALO + r1, rn), :], gbh.at[:, pl.ds(r0, rn), :],
                      s_gb.at[j], r_gb.at[j], 0, ds)

    for i, (df, ds) in enumerate(DIRS):
        @pl.when(valid(df, ds))
        def _(i=i, df=df, ds=ds):
            sky_copy(i, df, ds).start()
            if ds == 0:
                hw_copy(df).start()

    member = (lax.div(iota((chans, wide), 1), rows) == iota((chans, wide), 0))
    spread = lax.dot_general(w_ref[...], member.astype(BF16), (((0,), (0,)), ((), ())),
                             preferred_element_type=F32)
    masks = [band_mask(b, EDGE, rows, wide) for b in range(3)]
    for a in range(3):
        for e in range(3):
            tile = jnp.zeros((EDGE, wide), F32)
            for b in range(3):
                k = 9 * a + 3 * b + e
                tile = tile + jnp.where(masks[b], spread[k:k + 1, :], 0.0)
            bmat[pl.ds((3 * a + e) * EDGE, EDGE), :] = tile
    acc[...] = jnp.zeros(acc.shape, F32)

    def project(g, carry):
        pltpu.make_async_copy(cot_ref.at[:, g], cotv.at[g], cot_sem.at[g]).wait()
        res = jnp.dot(bmat[...].astype(BF16), cotv[g].reshape(wide, length),
                      preferred_element_type=F32)
        acc[pl.ds(g, 3)] += res.reshape(3, 3, EDGE, length)
        return carry

    lax.fori_loop(0, planes, project, 0)
    for p in range(planes + 2):
        total = acc[p, 1] + shift_next(acc[p, 0]) + shift_prev(acc[p, 2])
        part[p] = total
        ed[p:p + 1, :] = total[rows:rows + 1]
        eu[p:p + 1, :] = total[rows + 1:rows + 2]
    eu[planes + 2:, :] = jnp.zeros((8 - planes - 2, length), F32)
    ed[planes + 2:, :] = jnp.zeros((8 - planes - 2, length), F32)
    for i, (df, ds) in enumerate(DIRS):
        @pl.when(valid(df, ds))
        def _(i=i, df=df, ds=ds):
            part_copy(i, df, ds).start()

    for df in (-1, 1):
        @pl.when(valid(-df, 0))
        def _(df=df):
            hw_copy(df).wait_recv()

    def make_taps(p, carry):
        h = hwb[p]
        h2 = h * h

        def profile(d, reach, reach2):
            d = d.astype(F32)
            return jnp.where(jnp.abs(d) <= reach, jnp.exp(-2.0 * (d * d) / reach2), 0.0)

        lane = iota((8, 256), 1)
        small = jnp.where(lane <= 2 * MAXH, profile(lane - MAXH, h, h2), 0.0)
        inv = 1.0 / jnp.sqrt(jnp.sum(small * small, axis=1, keepdims=True))
        inv = jnp.broadcast_to(inv, (8, 256))[0:1]
        h, h2 = h[0:1], h2[0:1]
        shape = (3 * BLOCK, BLOCK)
        val = profile(iota(shape, 0) - BLOCK - iota(shape, 1), h[:, :BLOCK], h2[:, :BLOCK]) * inv[:, :BLOCK]
        hi = val.astype(BF16)
        tcol[p, :, 0:BLOCK] = hi
        tcol[p, :, BLOCK:] = (val - hi.astype(F32)).astype(BF16)
        shape = (BROWS, 256)
        lane = iota(shape, 1)
        row = row_of(iota(shape, 0), rows)
        val = profile(lax.rem(lane, tall) - HALO - row, h, h2) * inv
        hi = val.astype(BF16).astype(F32)
        trow[p] = jnp.where(lane < 2 * tall, hi, val - hi).astype(BF16)
        return carry

    lax.fori_loop(0, planes + 2, make_taps, 0)

    def blur(src, p, t, height):
        blocks = length // BLOCK
        field = jnp.concatenate(
            [src[p, :, j * BLOCK:(j + 3) * BLOCK] for j in range(blocks)], axis=0)
        both = jnp.dot(field, tcol[t], preferred_element_type=F32)
        q = both[:, :BLOCK] + both[:, BLOCK:]
        hi = q.astype(BF16)
        lo = (q - hi.astype(F32)).astype(BF16)
        hi = jnp.concatenate([hi[j * tall:(j + 1) * tall] for j in range(blocks)], axis=1)
        lo = jnp.concatenate([lo[j * tall:(j + 1) * tall] for j in range(blocks)], axis=1)
        return jnp.dot(trow[t][:height, :3 * tall], jnp.concatenate([hi, lo, hi], axis=0),
                       preferred_element_type=F32)

    own.wait()
    for i, (df, ds) in enumerate(DIRS):
        @pl.when(valid(-df, -ds))
        def _(i=i, df=df, ds=ds):
            sky_copy(i, df, ds).wait_recv()

    def make_beam(p, carry):
        beam = blur(skyh, p, p, BROWS)
        r = iota(beam.shape, 0)
        outside = jnp.logical_or(jnp.logical_and(r == rows, si == ns - 1),
                                 jnp.logical_and(r == rows + 1, si == 0))
        beam = jnp.where(outside, 0.0, beam)
        bs[p, 0] = shift_prev(beam).astype(BF16)
        bs[p, 1] = beam.astype(BF16)
        bs[p, 2] = shift_next(beam).astype(BF16)
        return carry

    lax.fori_loop(0, planes + 2, make_beam, 0)

    for i, (df, ds) in enumerate(DIRS):
        @pl.when(valid(-df, -ds))
        def _(i=i, df=df, ds=ds):
            part_copy(i, df, ds).wait_recv()
    r = iota((rows, length), 0)
    for f in range(planes):
        total = part[f + 1, 0:rows]
        if f == 0:
            total = total + pf[0]
        if f == planes - 1:
            total = total + pf[1]
        for up in (0, 1):
            line = pe[2 + up, f + 1:f + 2]
            if f == 0:
                line = line + pe[4 + up, planes + 1:planes + 2]
            if f == planes - 1:
                line = line + pe[up, 0:1]
            total = total + jnp.where(r == (0 if up else rows - 1), line, 0.0)
        gbh[f, HALO:HALO + rows, PAD:PAD + length] = total.astype(BF16)
    for ds in (-1, 1):
        @pl.when(valid(0, ds))
        def _(ds=ds):
            gb_copy(ds).start()

    def gram(g, total):
        left = bs[pl.ds(g, 3)].reshape(9 * BROWS, length)
        return total + lax.dot_general(left, cotv[g].reshape(wide, length),
                                       (((1,), (1,)), ((), ())), preferred_element_type=F32)

    acc2 = lax.fori_loop(0, planes, gram, jnp.zeros((9 * BROWS, wide), F32))
    masks = [band_mask(b, BROWS, rows, wide) for b in range(3)]
    lines = []
    for a in range(3):
        for b in range(3):
            for e in range(3):
                tile = acc2[(3 * a + e) * BROWS:(3 * a + e + 1) * BROWS]
                lines.append(jnp.sum(jnp.where(masks[b], tile, 0.0), axis=0, keepdims=True))
    lines.append(jnp.zeros((128 - 27, wide), F32))
    terms = lax.dot_general(member.astype(F32), jnp.concatenate(lines, axis=0),
                            (((1,), (1,)), ((), ())), precision=lax.Precision.HIGHEST,
                            preferred_element_type=F32)
    mine[...] = terms
    slots[si] = terms

    def kg_copy(k, src, dst, send, recv, at, size, axis):
        to = lax.rem(at + k, size)
        return pltpu.make_async_remote_copy(
            src_ref=src, dst_ref=dst.at[at], send_sem=send.at[k], recv_sem=recv.at[k],
            device_id=(to, si) if axis == 0 else (fi, to), device_id_type=MESH)

    def kg_wait(k, src, dst, send, recv, at, size, axis):
        pltpu.make_async_remote_copy(
            src_ref=src, dst_ref=dst.at[lax.rem(at - k + size, size)], send_sem=send.at[k],
            recv_sem=recv.at[k], device_id=(fi, si), device_id_type=MESH).wait_recv()

    over_sky = (mine, slots, s_kg, r_kg, si, ns, 1)
    over_freq = (mine2, slots2, s_kf, r_kf, fi, nf, 0)
    for k in range(1, ns):
        kg_copy(k, *over_sky).start()

    for ds in (-1, 1):
        @pl.when(valid(0, -ds))
        def _(ds=ds):
            gb_copy(ds).wait_recv()

    def finish(f, carry):
        out_ref[f] = blur(gbh, f, f + 1, rows)
        return carry

    lax.fori_loop(0, planes // 2, finish, 0)
    for k in range(1, ns):
        kg_wait(k, *over_sky)
    total = slots[0]
    for k in range(1, ns):
        total = total + slots[k]
    mine2[...] = total
    slots2[fi] = total
    for k in range(1, nf):
        kg_copy(k, *over_freq).start()
    lax.fori_loop(planes // 2, planes, finish, 0)
    for k in range(1, nf):
        kg_wait(k, *over_freq)
    total = slots2[0]
    for k in range(1, nf):
        total = total + slots2[k]
    kg_ref[...] = total[:, :27] * scale

    for i, (df, ds) in enumerate(DIRS):
        @pl.when(valid(df, ds))
        def _(i=i, df=df, ds=ds):
            sky_copy(i, df, ds).wait_send()
            part_copy(i, df, ds).wait_send()
            if ds == 0:
                hw_copy(df).wait_send()
            if df == 0:
                gb_copy(ds).wait_send()
    for k in range(1, ns):
        kg_copy(k, *over_sky).wait_send()
    for k in range(1, nf):
        kg_copy(k, *over_freq).wait_send()


def per_device(sky_cube, half_width, conv_weight, out_cotangent):
    planes, rows, length = sky_cube.shape
    chans = conv_weight.shape[0]
    nf, ns = lax.axis_size("freq"), lax.axis_size("sky")
    scale = 1.0 / math.sqrt(planes * nf * rows * ns * length)
    tall = rows + 2 * HALO
    wide = chans * rows
    dma = pltpu.SemaphoreType.DMA

    def kernel(*refs):
        body(nf, ns, scale, *refs)

    return pl.pallas_call(
        kernel,
        out_shape=(jax.ShapeDtypeStruct((planes, rows, length), F32),
                   jax.ShapeDtypeStruct((chans, 27), F32)),
        in_specs=[pl.BlockSpec(memory_space=pltpu.SMEM), pl.BlockSpec(memory_space=pl.ANY),
                  pl.BlockSpec(memory_space=pltpu.VMEM), pl.BlockSpec(memory_space=pl.ANY)],
        out_specs=(pl.BlockSpec(memory_space=pltpu.VMEM), pl.BlockSpec(memory_space=pltpu.VMEM)),
        scratch_shapes=[
            pltpu.VMEM((planes + 2, tall, length + 2 * PAD), BF16),
            pltpu.VMEM((planes, tall, length + 2 * PAD), BF16),
            pltpu.VMEM((planes, chans, rows, length), BF16),
            pltpu.VMEM((9 * EDGE, wide), F32),
            pltpu.VMEM((planes + 2, 3, EDGE, length), F32),
            pltpu.VMEM((planes + 2, EDGE, length), F32),
            pltpu.VMEM((8, length), F32),
            pltpu.VMEM((8, length), F32),
            pltpu.VMEM((2, rows, length), F32),
            pltpu.VMEM((6, 8, length), F32),
            pltpu.VMEM((planes + 2, 3, BROWS, length), BF16),
            pltpu.VMEM((planes + 2, 3 * BLOCK, 2 * BLOCK), BF16),
            pltpu.VMEM((planes + 2, BROWS, 256), BF16),
            pltpu.VMEM((planes + 2, 8, 256), F32),
            pltpu.VMEM((chans, 128), F32),
            pltpu.VMEM((ns, chans, 128), F32),
            pltpu.VMEM((chans, 128), F32),
            pltpu.VMEM((nf, chans, 128), F32),
            dma((planes,)), dma((1,)),
            dma((8,)), dma((8,)), dma((2,)), dma((2,)), dma((8,)), dma((8,)), dma((2,)), dma((2,)),
            dma((ns,)), dma((ns,)), dma((nf,)), dma((nf,)),
        ],
        compiler_params=pltpu.CompilerParams(
            collective_id=0, has_side_effects=True, vmem_limit_bytes=48 * 1024 * 1024),
        name="beam_backward",
    )(half_width, sky_cube, conv_weight, out_cotangent)


def solution(mesh):
    return jax.shard_map(
        per_device,
        mesh=mesh,
        in_specs=(P("freq", "sky", None), P("freq"), P(), P(None, "freq", "sky", None)),
        out_specs=(P("freq", "sky", None), P()),
        check_vma=False,
    )
```

profile of v0, /device:TPU:9, one launch (start us, length us, event | category | flops | bytes accessed | tf_op | source)
XLA Modules:
  0.0 40.5 jit_solution(7599991607703630185)
XLA Ops:
  0.6 0.0 copy-start
  0.6 2.2 %copy-done = bf16[16,4,32,1024]{3,2,1,0:T(8,128)(2,1)S(1)} copy-done((bf16[16,4,32,1024]{3,2,1,0:T(8,128)(2,1)S(1)}, bf16[16,4,32,1024]{3,2,1,0:T(8,128)(2,1)}, u32[]{:S(2)}) %copy-start) | copy-done | bytes 4194328
  2.8 0.0 copy-start.1
  2.8 0.9 %copy-done.1 = bf16[4,32,1024]{2,1,0:T(8,128)(2,1)S(1)} copy-done((bf16[4,32,1024]{2,1,0:T(8,128)(2,1)S(1)}, bf16[4,32,1024]{2,1,0:T(8,128)(2,1)}, u32[]{:S(2)}) %copy-start.1) | copy-done | bytes 262168
  3.8 0.0 copy-start.2
  3.8 0.7 %copy-done.2 = bf16[16,27]{1,0:T(8,128)(2,1)S(1)} copy-done((bf16[16,27]{1,0:T(8,128)(2,1)S(1)}, bf16[16,27]{1,0:T(8,128)(2,1)}, u32[]{:S(2)}) %copy-start.2) | copy-done | bytes 888
  4.5 0.0 copy-start.3
  4.5 0.7 %copy-done.3 = s32[4]{0:T(128)S(1)} copy-done((s32[4]{0:T(128)S(1)}, s32[4]{0:T(128)}, u32[]{:S(2)}) %copy-start.3) | copy-done | bytes 40
  5.1 34.0 %beam_backward.1 = (f32[4,32,1024]{2,1,0:T(8,128)S(1)}, f32[16,27]{1,0:T(8,128)S(1)}) custom-call(s32[4]{0:T(128)S(1)} %copy-done.3, bf16[4,32,1024]{2,1,0:T(8,128)(2,1)S(1)} %copy-done.1, bf16[16,27]{1,0:T(8,128)(2,1)S(1)} %copy-done.2, bf16[16,4,32,1024]{3,2,1,0:T(8,128)(2,1)S(1)} %copy-done), custom_call_target="tpu_custom_call" | custom-call | tf_op jit(solution)/shard_map/beam_backward/pallas_call | solution.py:371
  39.1 0.8 %copy.8 = f32[4,32,1024]{2,1,0:T(8,128)} copy(f32[4,32,1024]{2,1,0:T(8,128)S(1)} %get-tuple-element.4) | data formatting | bytes 1048576
  39.9 0.6 %copy.9 = f32[16,27]{1,0:T(8,128)} copy(f32[16,27]{1,0:T(8,128)S(1)} %get-tuple-element.5) | data formatting | bytes 3456
Async XLA Ops:
  0.6 2.2 %copy-start = (bf16[16,4,32,1024]{3,2,1,0:T(8,128)(2,1)S(1)}, bf16[16,4,32,1024]{3,2,1,0:T(8,128)(2,1)}, u32[]{:S(2)}) copy-start(bf16[16,4,32,1024]{3,2,1,0:T(8,128)(2,1)} %refs_3_.1) | copy-start | bytes 12582916
  2.8 0.9 %copy-start.1 = (bf16[4,32,1024]{2,1,0:T(8,128)(2,1)S(1)}, bf16[4,32,1024]{2,1,0:T(8,128)(2,1)}, u32[]{:S(2)}) copy-start(bf16[4,32,1024]{2,1,0:T(8,128)(2,1)} %refs_1_.1) | copy-start | bytes 786436
  3.8 0.7 %copy-start.2 = (bf16[16,27]{1,0:T(8,128)(2,1)S(1)}, bf16[16,27]{1,0:T(8,128)(2,1)}, u32[]{:S(2)}) copy-start(bf16[16,27]{1,0:T(8,128)(2,1)} %refs_2_.1) | copy-start | bytes 2596
  4.5 0.7 %copy-start.3 = (s32[4]{0:T(128)S(1)}, s32[4]{0:T(128)}, u32[]{:S(2)}) copy-start(s32[4]{0:T(128)} %refs_0_.1) | copy-start | bytes 52
where the time goes:
time: 40.8 us; the launch traced here: 40.5 us
  Pallas kernels  34 us (83%)
  local copies, waits for them, and re-layouts  5.87 us (14%)
  between operations  0.65 us (2%)
    pallas_call x1, Pallas kernels, per_device(): pl.pallas_call(kernel, out_shape=(jax.ShapeDtypeStruct((planes, rows, len...  34 us
    unnamed x10, local copies, waits for them, and re-layouts  5.87 us

commit v1 on v0

--- a/solution.py
+++ b/solution.py
@@ -13,6 +13,7 @@
 BLOCK = 128
 EDGE = 40
 BROWS = 48
+TALL3 = 128
 F32 = jnp.float32
 BF16 = jnp.bfloat16
 MESH = pl.DeviceIdType.MESH
@@ -42,8 +43,8 @@
     return jnp.where(iota(x.shape, 1) == 0, 0.0, pltpu.roll(x, 1, 1))
 
 
-def body(nf, ns, scale, hw_ref, sky_ref, w_ref, cot_ref, out_ref, kg_ref,
-         skyh, gbh, cotv, bmat, acc, part, eu, ed, pf, pe, bs, tcol, trow, hwb,
+def body(nf, ns, scale, hw_hbm, sky_ref, w_hbm, cot_ref, out_ref, kg_ref,
+         outv, out_sem, hw_ref, w_ref, skyh, gbh, cotv, bmat, acc, part, eu, ed, pf, pe, bs, tcol, trow, hwb,
          mine, slots, mine2, slots2,
          cot_sem, own_sem, s_sky, r_sky, s_hw, r_hw, s_part, r_part, s_gb, r_gb,
          s_kg, r_kg, s_kf, r_kf):
@@ -70,6 +71,10 @@
 
     lanes = pl.ds(PAD, length)
 
+    own_w = pltpu.make_async_copy(w_hbm, w_ref, own_sem.at[1])
+    own_w.start()
+    own_hw = pltpu.make_async_copy(hw_hbm, hw_ref, own_sem.at[2])
+    own_hw.start()
     cot_copies = [pltpu.make_async_copy(cot_ref.at[:, g], cotv.at[g], cot_sem.at[g])
                   for g in range(planes)]
     for copy in cot_copies:
@@ -77,12 +82,6 @@
     own = pltpu.make_async_copy(
         sky_ref, skyh.at[pl.ds(1, planes), pl.ds(HALO, rows), lanes], own_sem.at[0])
     own.start()
-    for ref in (skyh, gbh):
-        n = ref.shape[0]
-        ref[:, :, 0:PAD] = jnp.zeros((n, tall, PAD), BF16)
-        ref[:, :, PAD + length:] = jnp.zeros((n, tall, PAD), BF16)
-    for k in range(planes):
-        hwb[1 + k] = jnp.full((8, 256), hw_ref[k].astype(F32))
 
     def dst_sky(df, ds):
         p0, _, pn = span(df, 1, planes, 1, planes + 2)
@@ -118,6 +117,29 @@
             def _(df=df, ds=ds):
                 pl.semaphore_signal(barrier, inc=1, device_id=(fi + df, si + ds), device_id_type=MESH)
 
+    for ref in (skyh, gbh):
+        n = ref.shape[0]
+        ref[:, :, 0:PAD] = jnp.zeros((n, tall, PAD), BF16)
+        ref[:, :, PAD + length:] = jnp.zeros((n, tall, PAD), BF16)
+    own_hw.wait()
+    for k in range(planes):
+        hwb[1 + k] = jnp.full((8, 256), hw_ref[k].astype(F32))
+    own_w.wait()
+    member = (lax.div(iota((chans, wide), 1), rows) == iota((chans, wide), 0))
+    spread = lax.dot_general(w_ref[...], member.astype(BF16), (((0,), (0,)), ((), ())),
+                             preferred_element_type=F32)
+    masks = [band_mask(b, EDGE, rows, wide) for b in range(3)]
+    tiles = []
+    for a in range(3):
+        for e in range(3):
+            tile = jnp.zeros((EDGE, wide), F32)
+            for b in range(3):
+                k = 9 * a + 3 * b + e
+                tile = tile + jnp.where(masks[b], spread[k:k + 1, :], 0.0)
+            tiles.append(tile)
+    tiles.append(jnp.zeros((8, wide), F32))
+    bmat[...] = jnp.concatenate(tiles, axis=0).astype(BF16)
+
     pl.semaphore_wait(barrier, greeted)
 
     def remote(src, dst, send, recv, df, ds):
@@ -156,32 +178,24 @@
             if ds == 0:
                 hw_copy(df).start()
 
-    member = (lax.div(iota((chans, wide), 1), rows) == iota((chans, wide), 0))
-    spread = lax.dot_general(w_ref[...], member.astype(BF16), (((0,), (0,)), ((), ())),
-                             preferred_element_type=F32)
-    masks = [band_mask(b, EDGE, rows, wide) for b in range(3)]
-    for a in range(3):
-        for e in range(3):
-            tile = jnp.zeros((EDGE, wide), F32)
-            for b in range(3):
-                k = 9 * a + 3 * b + e
-                tile = tile + jnp.where(masks[b], spread[k:k + 1, :], 0.0)
-            bmat[pl.ds((3 * a + e) * EDGE, EDGE), :] = tile
-    acc[...] = jnp.zeros(acc.shape, F32)
-
-    def project(g, carry):
-        pltpu.make_async_copy(cot_ref.at[:, g], cotv.at[g], cot_sem.at[g]).wait()
-        res = jnp.dot(bmat[...].astype(BF16), cotv[g].reshape(wide, length),
-                      preferred_element_type=F32)
-        acc[pl.ds(g, 3)] += res.reshape(3, 3, EDGE, length)
-        return carry
-
-    lax.fori_loop(0, planes, project, 0)
-    for p in range(planes + 2):
+    def close_plane(p):
         total = acc[p, 1] + shift_next(acc[p, 0]) + shift_prev(acc[p, 2])
         part[p] = total
         ed[p:p + 1, :] = total[rows:rows + 1]
         eu[p:p + 1, :] = total[rows + 1:rows + 2]
+
+    for g in range(planes):
+        cot_copies[g].wait()
+        res = jnp.dot(bmat[...], cotv[g].reshape(wide, length), preferred_element_type=F32)
+        for a in range(3):
+            piece = res[3 * a * EDGE:3 * (a + 1) * EDGE].reshape(3, EDGE, length)
+            if g == 0 or a == 2:
+                acc[g + a] = piece
+            else:
+                acc[g + a] += piece
+        close_plane(g)
+    close_plane(planes)
+    close_plane(planes + 1)
     eu[planes + 2:, :] = jnp.zeros((8 - planes - 2, length), F32)
     ed[planes + 2:, :] = jnp.zeros((8 - planes - 2, length), F32)
     for i, (df, ds) in enumerate(DIRS):
@@ -194,7 +208,7 @@
         def _(df=df):
             hw_copy(df).wait_recv()
 
-    def make_taps(p, carry):
+    def make_taps(p):
         h = hwb[p]
         h2 = h * h
 
@@ -218,9 +232,9 @@
         val = profile(lax.rem(lane, tall) - HALO - row, h, h2) * inv
         hi = val.astype(BF16).astype(F32)
         trow[p] = jnp.where(lane < 2 * tall, hi, val - hi).astype(BF16)
-        return carry
-
-    lax.fori_loop(0, planes + 2, make_taps, 0)
+
+    for p in range(planes + 2):
+        make_taps(p)
 
     def blur(src, p, t, height):
         blocks = length // BLOCK
@@ -241,18 +255,15 @@
         def _(i=i, df=df, ds=ds):
             sky_copy(i, df, ds).wait_recv()
 
-    def make_beam(p, carry):
-        beam = blur(skyh, p, p, BROWS)
+    for p in range(planes + 2):
+        beam = blur(skyh, p, p, BROWS)[:EDGE]
         r = iota(beam.shape, 0)
         outside = jnp.logical_or(jnp.logical_and(r == rows, si == ns - 1),
                                  jnp.logical_and(r == rows + 1, si == 0))
         beam = jnp.where(outside, 0.0, beam)
-        bs[p, 0] = shift_prev(beam).astype(BF16)
-        bs[p, 1] = beam.astype(BF16)
-        bs[p, 2] = shift_next(beam).astype(BF16)
-        return carry
-
-    lax.fori_loop(0, planes + 2, make_beam, 0)
+        bs[p] = jnp.concatenate(
+            [shift_prev(beam), beam, shift_next(beam), jnp.zeros((8, length), F32)],
+            axis=0).astype(BF16)
 
     for i, (df, ds) in enumerate(DIRS):
         @pl.when(valid(-df, -ds))
@@ -278,25 +289,25 @@
         def _(ds=ds):
             gb_copy(ds).start()
 
-    def gram(g, total):
-        left = bs[pl.ds(g, 3)].reshape(9 * BROWS, length)
-        return total + lax.dot_general(left, cotv[g].reshape(wide, length),
-                                       (((1,), (1,)), ((), ())), preferred_element_type=F32)
-
-    acc2 = lax.fori_loop(0, planes, gram, jnp.zeros((9 * BROWS, wide), F32))
-    masks = [band_mask(b, BROWS, rows, wide) for b in range(3)]
+    acc2 = jnp.zeros((3 * TALL3, wide), F32)
+    for g in range(planes):
+        acc2 = acc2 + lax.dot_general(
+            bs[g:g + 3].reshape(3 * TALL3, length), cotv[g].reshape(wide, length),
+            (((1,), (1,)), ((), ())), preferred_element_type=F32)
     lines = []
     for a in range(3):
         for b in range(3):
             for e in range(3):
-                tile = acc2[(3 * a + e) * BROWS:(3 * a + e + 1) * BROWS]
+                tile = acc2[a * TALL3 + e * EDGE:a * TALL3 + (e + 1) * EDGE]
                 lines.append(jnp.sum(jnp.where(masks[b], tile, 0.0), axis=0, keepdims=True))
     lines.append(jnp.zeros((128 - 27, wide), F32))
     terms = lax.dot_general(member.astype(F32), jnp.concatenate(lines, axis=0),
                             (((1,), (1,)), ((), ())), precision=lax.Precision.HIGHEST,
                             preferred_element_type=F32)
-    mine[...] = terms
-    slots[si] = terms
+    half = chans // 2
+    packed = terms[:half] + pltpu.roll(terms[half:], 64, 1)
+    mine[...] = packed
+    slots[si] = packed
 
     def kg_copy(k, src, dst, send, recv, at, size, axis):
         to = lax.rem(at + k, size)
@@ -319,11 +330,15 @@
         def _(ds=ds):
             gb_copy(ds).wait_recv()
 
-    def finish(f, carry):
-        out_ref[f] = blur(gbh, f, f + 1, rows)
-        return carry
-
-    lax.fori_loop(0, planes // 2, finish, 0)
+    out_copies = [pltpu.make_async_copy(outv.at[f], out_ref.at[f], out_sem.at[f])
+                  for f in range(planes)]
+
+    def finish(f):
+        outv[f] = blur(gbh, f, f + 1, rows)
+        out_copies[f].start()
+
+    for f in range(planes // 2):
+        finish(f)
     for k in range(1, ns):
         kg_wait(k, *over_sky)
     total = slots[0]
@@ -333,14 +348,19 @@
     slots2[fi] = total
     for k in range(1, nf):
         kg_copy(k, *over_freq).start()
-    lax.fori_loop(planes // 2, planes, finish, 0)
+    for f in range(planes // 2, planes):
+        finish(f)
     for k in range(1, nf):
         kg_wait(k, *over_freq)
     total = slots2[0]
     for k in range(1, nf):
         total = total + slots2[k]
-    kg_ref[...] = total[:, :27] * scale
-
+    total = total * scale
+    kg_ref[0:half] = total[:, :27]
+    kg_ref[half:] = pltpu.roll(total, 64, 1)[:, :27]
+
+    for copy in out_copies:
+        copy.wait()
     for i, (df, ds) in enumerate(DIRS):
         @pl.when(valid(df, ds))
         def _(i=i, df=df, ds=ds):
@@ -372,34 +392,36 @@
         kernel,
         out_shape=(jax.ShapeDtypeStruct((planes, rows, length), F32),
                    jax.ShapeDtypeStruct((chans, 27), F32)),
-        in_specs=[pl.BlockSpec(memory_space=pltpu.SMEM), pl.BlockSpec(memory_space=pl.ANY),
-                  pl.BlockSpec(memory_space=pltpu.VMEM), pl.BlockSpec(memory_space=pl.ANY)],
-        out_specs=(pl.BlockSpec(memory_space=pltpu.VMEM), pl.BlockSpec(memory_space=pltpu.VMEM)),
+        in_specs=[pl.BlockSpec(memory_space=pltpu.HBM)] * 4,
+        out_specs=(pl.BlockSpec(memory_space=pltpu.HBM), pl.BlockSpec(memory_space=pltpu.VMEM)),
         scratch_shapes=[
+            pltpu.VMEM((planes, rows, length), F32), dma((planes,)),
+            pltpu.SMEM((planes,), jnp.int32),
+            pltpu.VMEM((chans, 27), BF16),
             pltpu.VMEM((planes + 2, tall, length + 2 * PAD), BF16),
             pltpu.VMEM((planes, tall, length + 2 * PAD), BF16),
             pltpu.VMEM((planes, chans, rows, length), BF16),
-            pltpu.VMEM((9 * EDGE, wide), F32),
+            pltpu.VMEM((9 * EDGE + 8, wide), BF16),
             pltpu.VMEM((planes + 2, 3, EDGE, length), F32),
             pltpu.VMEM((planes + 2, EDGE, length), F32),
             pltpu.VMEM((8, length), F32),
             pltpu.VMEM((8, length), F32),
             pltpu.VMEM((2, rows, length), F32),
             pltpu.VMEM((6, 8, length), F32),
-            pltpu.VMEM((planes + 2, 3, BROWS, length), BF16),
+            pltpu.VMEM((planes + 2, TALL3, length), BF16),
             pltpu.VMEM((planes + 2, 3 * BLOCK, 2 * BLOCK), BF16),
             pltpu.VMEM((planes + 2, BROWS, 256), BF16),
             pltpu.VMEM((planes + 2, 8, 256), F32),
-            pltpu.VMEM((chans, 128), F32),
-            pltpu.VMEM((ns, chans, 128), F32),
-            pltpu.VMEM((chans, 128), F32),
-            pltpu.VMEM((nf, chans, 128), F32),
-            dma((planes,)), dma((1,)),
+            pltpu.VMEM((chans // 2, 128), F32),
+            pltpu.VMEM((ns, chans // 2, 128), F32),
+            pltpu.VMEM((chans // 2, 128), F32),
+            pltpu.VMEM((nf, chans // 2, 128), F32),
+            dma((planes,)), dma((3,)),
             dma((8,)), dma((8,)), dma((2,)), dma((2,)), dma((8,)), dma((8,)), dma((2,)), dma((2,)),
             dma((ns,)), dma((ns,)), dma((nf,)), dma((nf,)),
         ],
         compiler_params=pltpu.CompilerParams(
-            collective_id=0, has_side_effects=True, vmem_limit_bytes=48 * 1024 * 1024),
+            collective_id=0, has_side_effects=True, vmem_limit_bytes=60 * 1024 * 1024),
         name="beam_backward",
     )(half_width, sky_cube, conv_weight, out_cotangent)
 

time: 40.8 us -> 36.9 us (0.904)
  local copies, waits for them, and re-layouts: 5.87 us -> 3.18 us
  Pallas kernels: 34 us -> 32.9 us
    unnamed x10 -> x2, local copies, waits for them, and re-layouts: 5.87 us -> 3.18 us
    pallas_call x1, Pallas kernels: 34 us -> 32.9 us  [per_device(): pl.pallas_call(kernel, out_shape=(jax.ShapeDtypeStruct((planes, rows, len...]
where the time goes in v1:
time: 36.9 us; the launch traced here: 36.7 us
  Pallas kernels  32.9 us (89%)
  local copies, waits for them, and re-layouts  3.18 us (9%)
  between operations  0.64 us (2%)
    pallas_call x1, Pallas kernels, per_device(): pl.pallas_call(kernel, out_shape=(jax.ShapeDtypeStruct((planes, rows, len...  32.9 us
    unnamed x2, local copies, waits for them, and re-layouts  3.18 us

profile of v1, /device:TPU:9, one launch (start us, length us, event | category | flops | bytes accessed | tf_op | source)
XLA Modules:
  0.0 36.7 jit_solution(14710192865303128208)
XLA Ops:
  0.6 32.9 %beam_backward.1 = (f32[4,32,1024]{2,1,0:T(8,128)}, f32[16,27]{1,0:T(8,128)}) custom-call(s32[4]{0:T(128)} %refs_0_.1, bf16[4,32,1024]{2,1,0:T(8,128)(2,1)} %refs_1_.1, bf16[16,27]{1,0:T(8,128)(2,1)} %refs_2_.1, bf16[16,4,32,1024]{3,2,1,0:T(8,128)(2,1)} %refs_3_.1), custom_call_target="tpu_custom_call" | custom-call | tf_op jit(solution)/shard_map/beam_backward/pallas_call | solution.py:391
  33.5 1.9 %copy.8 = f32[4,32,1024]{2,1,0:T(8,128)} copy(f32[4,32,1024]{2,1,0:T(8,128)} %get-tuple-element.4) | data formatting | bytes 1048576
  35.4 1.3 %copy.9 = f32[16,27]{1,0:T(8,128)} copy(f32[16,27]{1,0:T(8,128)} %get-tuple-element.5) | data formatting | bytes 3456

commit v2 on v1

--- a/solution.py
+++ b/solution.py
@@ -11,9 +11,9 @@
 HALO = 16
 PAD = 128
 BLOCK = 128
-EDGE = 40
-BROWS = 48
-TALL3 = 128
+HALF = 16
+EDGE = 24
+TALL3 = 80
 F32 = jnp.float32
 BF16 = jnp.bfloat16
 MESH = pl.DeviceIdType.MESH
@@ -50,7 +50,9 @@
          s_kg, r_kg, s_kf, r_kf):
     planes, rows, length = out_ref.shape
     chans = w_ref.shape[0]
-    wide = chans * rows
+    wide = chans * HALF
+    halves = rows // HALF
+    high = halves * EDGE
     tall = rows + 2 * HALO
     fi, si = lax.axis_index("freq"), lax.axis_index("sky")
 
@@ -125,10 +127,10 @@
     for k in range(planes):
         hwb[1 + k] = jnp.full((8, 256), hw_ref[k].astype(F32))
     own_w.wait()
-    member = (lax.div(iota((chans, wide), 1), rows) == iota((chans, wide), 0))
+    member = (lax.div(iota((chans, wide), 1), HALF) == iota((chans, wide), 0))
     spread = lax.dot_general(w_ref[...], member.astype(BF16), (((0,), (0,)), ((), ())),
                              preferred_element_type=F32)
-    masks = [band_mask(b, EDGE, rows, wide) for b in range(3)]
+    masks = [band_mask(b, EDGE, HALF, wide) for b in range(3)]
     tiles = []
     for a in range(3):
         for e in range(3):
@@ -178,21 +180,33 @@
             if ds == 0:
                 hw_copy(df).start()
 
+    def cot_half(g, h):
+        return cotv[g, :, h * HALF:(h + 1) * HALF, :].reshape(wide, length)
+
     def close_plane(p):
-        total = acc[p, 1] + shift_next(acc[p, 0]) + shift_prev(acc[p, 2])
-        part[p] = total
-        ed[p:p + 1, :] = total[rows:rows + 1]
-        eu[p:p + 1, :] = total[rows + 1:rows + 2]
+        r = iota((HALF, length), 0)
+        piece = [acc[p, h, 1] + shift_next(acc[p, h, 0]) + shift_prev(acc[p, h, 2])
+                 for h in range(halves)]
+        for h in range(halves):
+            total = piece[h][:HALF]
+            if h > 0:
+                total = total + jnp.where(r == 0, piece[h - 1][HALF:HALF + 1], 0.0)
+            if h < halves - 1:
+                total = total + jnp.where(r == HALF - 1, piece[h + 1][HALF + 1:HALF + 2], 0.0)
+            part[p, h * HALF:(h + 1) * HALF] = total
+        ed[p:p + 1, :] = piece[-1][HALF:HALF + 1]
+        eu[p:p + 1, :] = piece[0][HALF + 1:HALF + 2]
 
     for g in range(planes):
         cot_copies[g].wait()
-        res = jnp.dot(bmat[...], cotv[g].reshape(wide, length), preferred_element_type=F32)
-        for a in range(3):
-            piece = res[3 * a * EDGE:3 * (a + 1) * EDGE].reshape(3, EDGE, length)
-            if g == 0 or a == 2:
-                acc[g + a] = piece
-            else:
-                acc[g + a] += piece
+        for h in range(halves):
+            res = jnp.dot(bmat[...], cot_half(g, h), preferred_element_type=F32)
+            for a in range(3):
+                piece = res[3 * a * EDGE:3 * (a + 1) * EDGE].reshape(3, EDGE, length)
+                if g == 0 or a == 2:
+                    acc[g + a, h] = piece
+                else:
+                    acc[g + a, h] += piece
         close_plane(g)
     close_plane(planes)
     close_plane(planes + 1)
@@ -226,9 +240,9 @@
         hi = val.astype(BF16)
         tcol[p, :, 0:BLOCK] = hi
         tcol[p, :, BLOCK:] = (val - hi.astype(F32)).astype(BF16)
-        shape = (BROWS, 256)
+        shape = (high, 256)
         lane = iota(shape, 1)
-        row = row_of(iota(shape, 0), rows)
+        row = row_of(lax.rem(iota(shape, 0), EDGE), HALF) + HALF * lax.div(iota(shape, 0), EDGE)
         val = profile(lax.rem(lane, tall) - HALO - row, h, h2) * inv
         hi = val.astype(BF16).astype(F32)
         trow[p] = jnp.where(lane < 2 * tall, hi, val - hi).astype(BF16)
@@ -236,7 +250,7 @@
     for p in range(planes + 2):
         make_taps(p)
 
-    def blur(src, p, t, height):
+    def blur(src, p, t):
         blocks = length // BLOCK
         field = jnp.concatenate(
             [src[p, :, j * BLOCK:(j + 3) * BLOCK] for j in range(blocks)], axis=0)
@@ -246,7 +260,7 @@
         lo = (q - hi.astype(F32)).astype(BF16)
         hi = jnp.concatenate([hi[j * tall:(j + 1) * tall] for j in range(blocks)], axis=1)
         lo = jnp.concatenate([lo[j * tall:(j + 1) * tall] for j in range(blocks)], axis=1)
-        return jnp.dot(trow[t][:height, :3 * tall], jnp.concatenate([hi, lo, hi], axis=0),
+        return jnp.dot(trow[t][:, :3 * tall], jnp.concatenate([hi, lo, hi], axis=0),
                        preferred_element_type=F32)
 
     own.wait()
@@ -256,14 +270,16 @@
             sky_copy(i, df, ds).wait_recv()
 
     for p in range(planes + 2):
-        beam = blur(skyh, p, p, BROWS)[:EDGE]
+        beam = blur(skyh, p, p)
         r = iota(beam.shape, 0)
-        outside = jnp.logical_or(jnp.logical_and(r == rows, si == ns - 1),
-                                 jnp.logical_and(r == rows + 1, si == 0))
+        outside = jnp.logical_or(jnp.logical_and(r == high - EDGE + HALF, si == ns - 1),
+                                 jnp.logical_and(r == HALF + 1, si == 0))
         beam = jnp.where(outside, 0.0, beam)
-        bs[p] = jnp.concatenate(
-            [shift_prev(beam), beam, shift_next(beam), jnp.zeros((8, length), F32)],
-            axis=0).astype(BF16)
+        shifts = (shift_prev(beam), beam, shift_next(beam))
+        for h in range(halves):
+            bs[h, p] = jnp.concatenate(
+                [x[h * EDGE:(h + 1) * EDGE] for x in shifts] + [jnp.zeros((8, length), F32)],
+                axis=0).astype(BF16)
 
     for i, (df, ds) in enumerate(DIRS):
         @pl.when(valid(-df, -ds))
@@ -291,9 +307,10 @@
 
     acc2 = jnp.zeros((3 * TALL3, wide), F32)
     for g in range(planes):
-        acc2 = acc2 + lax.dot_general(
-            bs[g:g + 3].reshape(3 * TALL3, length), cotv[g].reshape(wide, length),
-            (((1,), (1,)), ((), ())), preferred_element_type=F32)
+        for h in range(halves):
+            acc2 = acc2 + lax.dot_general(
+                bs[h, g:g + 3].reshape(3 * TALL3, length), cot_half(g, h),
+                (((1,), (1,)), ((), ())), preferred_element_type=F32)
     lines = []
     for a in range(3):
         for b in range(3):
@@ -334,7 +351,9 @@
                   for f in range(planes)]
 
     def finish(f):
-        outv[f] = blur(gbh, f, f + 1, rows)
+        both = blur(gbh, f, f + 1)
+        for h in range(halves):
+            outv[f, h * HALF:(h + 1) * HALF] = both[h * EDGE:h * EDGE + HALF]
         out_copies[f].start()
 
     for f in range(planes // 2):
@@ -355,9 +374,7 @@
     total = slots2[0]
     for k in range(1, nf):
         total = total + slots2[k]
-    total = total * scale
-    kg_ref[0:half] = total[:, :27]
-    kg_ref[half:] = pltpu.roll(total, 64, 1)[:, :27]
+    kg_ref[...] = total * scale
 
     for copy in out_copies:
         copy.wait()
@@ -376,22 +393,37 @@
         kg_copy(k, *over_freq).wait_send()
 
 
+def hand_on(sky_ref, packed_ref, out_ref, kg_ref, sems):
+    copies = [pltpu.make_async_copy(sky_ref.at[f], out_ref.at[f], sems.at[f])
+              for f in range(sky_ref.shape[0])]
+    for copy in copies:
+        copy.start()
+    packed = packed_ref[...]
+    half = packed.shape[0]
+    kg_ref[0:half] = packed[:, :27]
+    kg_ref[half:] = pltpu.roll(packed, 64, 1)[:, :27]
+    for copy in copies:
+        copy.wait()
+
+
 def per_device(sky_cube, half_width, conv_weight, out_cotangent):
     planes, rows, length = sky_cube.shape
     chans = conv_weight.shape[0]
     nf, ns = lax.axis_size("freq"), lax.axis_size("sky")
     scale = 1.0 / math.sqrt(planes * nf * rows * ns * length)
     tall = rows + 2 * HALO
-    wide = chans * rows
+    wide = chans * HALF
+    halves = rows // HALF
+    high = halves * EDGE
     dma = pltpu.SemaphoreType.DMA
 
     def kernel(*refs):
         body(nf, ns, scale, *refs)
 
-    return pl.pallas_call(
+    sky_grad, packed = pl.pallas_call(
         kernel,
         out_shape=(jax.ShapeDtypeStruct((planes, rows, length), F32),
-                   jax.ShapeDtypeStruct((chans, 27), F32)),
+                   jax.ShapeDtypeStruct((chans // 2, 128), F32)),
         in_specs=[pl.BlockSpec(memory_space=pltpu.HBM)] * 4,
         out_specs=(pl.BlockSpec(memory_space=pltpu.HBM), pl.BlockSpec(memory_space=pltpu.VMEM)),
         scratch_shapes=[
@@ -402,15 +434,15 @@
             pltpu.VMEM((planes, tall, length + 2 * PAD), BF16),
             pltpu.VMEM((planes, chans, rows, length), BF16),
             pltpu.VMEM((9 * EDGE + 8, wide), BF16),
-            pltpu.VMEM((planes + 2, 3, EDGE, length), F32),
-            pltpu.VMEM((planes + 2, EDGE, length), F32),
+            pltpu.VMEM((planes + 2, halves, 3, EDGE, length), F32),
+            pltpu.VMEM((planes + 2, rows, length), F32),
             pltpu.VMEM((8, length), F32),
             pltpu.VMEM((8, length), F32),
             pltpu.VMEM((2, rows, length), F32),
             pltpu.VMEM((6, 8, length), F32),
-            pltpu.VMEM((planes + 2, TALL3, length), BF16),
+            pltpu.VMEM((halves, planes + 2, TALL3, length), BF16),
             pltpu.VMEM((planes + 2, 3 * BLOCK, 2 * BLOCK), BF16),
-            pltpu.VMEM((planes + 2, BROWS, 256), BF16),
+            pltpu.VMEM((planes + 2, high, 256), BF16),
             pltpu.VMEM((planes + 2, 8, 256), F32),
             pltpu.VMEM((chans // 2, 128), F32),
             pltpu.VMEM((ns, chans // 2, 128), F32),
@@ -424,6 +456,16 @@
             collective_id=0, has_side_effects=True, vmem_limit_bytes=60 * 1024 * 1024),
         name="beam_backward",
     )(half_width, sky_cube, conv_weight, out_cotangent)
+    return pl.pallas_call(
+        hand_on,
+        out_shape=(jax.ShapeDtypeStruct((planes, rows, length), F32),
+                   jax.ShapeDtypeStruct((chans, 27), F32)),
+        in_specs=[pl.BlockSpec(memory_space=pltpu.HBM), pl.BlockSpec(memory_space=pltpu.VMEM)],
+        out_specs=(pl.BlockSpec(memory_space=pltpu.HBM), pl.BlockSpec(memory_space=pltpu.VMEM)),
+        scratch_shapes=[dma((planes,))],
+        compiler_params=pltpu.CompilerParams(vmem_limit_bytes=60 * 1024 * 1024),
+        name="hand_on",
+    )(sky_grad, packed)
 
 
 def solution(mesh):

time: 36.9 us -> 51.6 us (1.40)
  Pallas kernels: 32.9 us -> 50.8 us
  local copies, waits for them, and re-layouts: 3.18 us -> 0 us
    pallas_call x0 -> x1, Pallas kernels: none -> 18.3 us  [per_device(): pl.pallas_call(hand_on, out_shape=(jax.ShapeDtypeStruct((planes, rows, le...]
    unnamed x2 -> x0, local copies, waits for them, and re-layouts: 3.18 us -> none
where the time goes in v2:
time: 51.6 us; the launch traced here: 51.4 us
  Pallas kernels  50.8 us (98%)
  between operations  0.64 us (1%)
    pallas_call x1, Pallas kernels, per_device(): pl.pallas_call(kernel, out_shape=(jax.ShapeDtypeStruct((planes, rows, len...  32.5 us
    pallas_call x1, Pallas kernels, per_device(): pl.pallas_call(hand_on, out_shape=(jax.ShapeDtypeStruct((planes, rows, le...  18.3 us

profile of v2, /device:TPU:9, one launch (start us, length us, event | category | flops | bytes accessed | tf_op | source)
XLA Modules:
  0.0 51.4 jit_solution(3236491914853682876)
XLA Ops:
  0.6 32.5 %beam_backward.1 = (f32[4,32,1024]{2,1,0:T(8,128)}, f32[8,128]{1,0:T(8,128)}) custom-call(s32[4]{0:T(128)} %refs_0_.1, bf16[4,32,1024]{2,1,0:T(8,128)(2,1)} %refs_1_.1, bf16[16,27]{1,0:T(8,128)(2,1)} %refs_2_.1, bf16[16,4,32,1024]{3,2,1,0:T(8,128)(2,1)} %refs_3_.1), custom_call_target="tpu_custom_call" | custom-call | tf_op jit(solution)/shard_map/beam_backward/pallas_call | solution.py:423
  33.2 18.3 %hand_on.1 = (f32[4,32,1024]{2,1,0:T(8,128)}, f32[16,27]{1,0:T(8,128)}) custom-call(f32[4,32,1024]{2,1,0:T(8,128)} %get-tuple-element.4.sky_ref, f32[8,128]{1,0:T(8,128)} %get-tuple-element.5.packed_ref), custom_call_target="tpu_custom_call" | custom-call | tf_op jit(solution)/shard_map/hand_on/pallas_call | solution.py:459

commit v3 on v2

--- a/solution.py
+++ b/solution.py
@@ -44,9 +44,9 @@
 
 
 def body(nf, ns, scale, hw_hbm, sky_ref, w_hbm, cot_ref, out_ref, kg_ref,
-         outv, out_sem, hw_ref, w_ref, skyh, gbh, cotv, bmat, acc, part, eu, ed, pf, pe, bs, tcol, trow, hwb,
-         mine, slots, mine2, slots2,
-         cot_sem, own_sem, s_sky, r_sky, s_hw, r_hw, s_part, r_part, s_gb, r_gb,
+         outv, out_sem, hw_ref, w_ref, skyh, gbh, cotv, bmat, acc, part, eu, ed, pf, pe, pc,
+         bm, bs, tcol, trow, hwb, mine, slots, mine2, slots2,
+         cot_sem, own_sem, s_sky, r_sky, s_part, r_part, s_gb, r_gb, s_bm, r_bm,
          s_kg, r_kg, s_kf, r_kf):
     planes, rows, length = out_ref.shape
     chans = w_ref.shape[0]
@@ -72,6 +72,7 @@
         return own_lo + own_n, 0, halo_n
 
     lanes = pl.ds(PAD, length)
+    order = [0, planes - 1] + list(range(1, planes - 1))
 
     own_w = pltpu.make_async_copy(w_hbm, w_ref, own_sem.at[1])
     own_w.start()
@@ -82,27 +83,23 @@
     for copy in cot_copies:
         copy.start()
     own = pltpu.make_async_copy(
-        sky_ref, skyh.at[pl.ds(1, planes), pl.ds(HALO, rows), lanes], own_sem.at[0])
+        sky_ref, skyh.at[:, pl.ds(HALO, rows), lanes], own_sem.at[0])
     own.start()
 
-    def dst_sky(df, ds):
-        p0, _, pn = span(df, 1, planes, 1, planes + 2)
-        r0, _, rn = span(ds, HALO, rows, HALO, tall)
-        return skyh.at[pl.ds(p0, pn), pl.ds(r0, rn), lanes]
-
-    for i, (df, ds) in enumerate(DIRS):
+    for df, ds in DIRS:
         @pl.when(jnp.logical_not(valid(-df, -ds)))
         def _(df=df, ds=ds):
-            ref = dst_sky(df, ds)
-            ref[...] = jnp.zeros(ref.shape, BF16)
             if df == 0:
                 r0, _, rn = span(ds, HALO, rows, HALO, tall)
-                gbh[:, r0:r0 + rn, PAD:PAD + length] = jnp.zeros((planes, rn, length), BF16)
-            if ds == 0:
-                hwb[0 if df > 0 else planes + 1] = jnp.ones((8, 256), F32)
+                zero = jnp.zeros((planes, rn, length), BF16)
+                skyh[:, r0:r0 + rn, PAD:PAD + length] = zero
+                gbh[:, r0:r0 + rn, PAD:PAD + length] = zero
+                pe[0 if ds < 0 else 1] = jnp.zeros((planes, 8, length // 8), F32)
+            elif ds == 0:
+                bm[0 if df > 0 else planes + 1] = jnp.zeros((high, length), BF16)
                 pf[0 if df > 0 else 1] = jnp.zeros((rows, length), F32)
             else:
-                pe[(df + 1) * 2 + (ds > 0)] = jnp.zeros((8, length), F32)
+                pc[(df > 0) * 2 + (ds > 0)] = jnp.zeros((1, 8, length // 8), F32)
 
     barrier = pltpu.get_barrier_semaphore()
     for k in range(1, ns):
@@ -125,7 +122,7 @@
         ref[:, :, PAD + length:] = jnp.zeros((n, tall, PAD), BF16)
     own_hw.wait()
     for k in range(planes):
-        hwb[1 + k] = jnp.full((8, 256), hw_ref[k].astype(F32))
+        hwb[k] = jnp.full((8, 256), hw_ref[k].astype(F32))
     own_w.wait()
     member = (lax.div(iota((chans, wide), 1), HALF) == iota((chans, wide), 0))
     spread = lax.dot_general(w_ref[...], member.astype(BF16), (((0,), (0,)), ((), ())),
@@ -149,36 +146,40 @@
             src_ref=src, dst_ref=dst, send_sem=send, recv_sem=recv,
             device_id=(fi + df, si + ds), device_id_type=MESH)
 
-    def sky_copy(i, df, ds):
-        _, p0, pn = span(df, 1, planes, 1, planes + 2)
-        _, r0, rn = span(ds, HALO, rows, HALO, tall)
-        return remote(sky_ref.at[pl.ds(p0, pn), pl.ds(r0, rn), :], dst_sky(df, ds),
-                      s_sky.at[i], r_sky.at[i], df, ds)
-
-    def hw_copy(df):
+    def halo_copy(ref, send, recv, ds, f):
+        i = (ds > 0) * planes + f
+        r0, r1, rn = span(ds, HALO, rows, HALO, tall)
+        return remote(ref.at[f, pl.ds(HALO + r1, rn), lanes], ref.at[f, pl.ds(r0, rn), lanes],
+                      send.at[i], recv.at[i], 0, ds)
+
+    def sky_copy(ds, f):
+        return halo_copy(skyh, s_sky, r_sky, ds, f)
+
+    def gb_copy(ds, f):
+        return halo_copy(gbh, s_gb, r_gb, ds, f)
+
+    def bm_copy(df):
         j = 0 if df > 0 else 1
-        return remote(hwb.at[planes if df > 0 else 1], hwb.at[0 if df > 0 else planes + 1],
-                      s_hw.at[j], r_hw.at[j], df, 0)
+        return remote(bm.at[planes if df > 0 else 1], bm.at[0 if df > 0 else planes + 1],
+                      s_bm.at[j], r_bm.at[j], df, 0)
 
     def part_copy(i, df, ds):
+        edge = ed if ds > 0 else eu
         if ds == 0:
-            src, dst = part.at[planes + 1 if df > 0 else 0, pl.ds(0, rows)], pf.at[0 if df > 0 else 1]
+            src, dst = part.at[planes + 1 if df > 0 else 0], pf.at[0 if df > 0 else 1]
+        elif df == 0:
+            src, dst = edge.at[pl.ds(1, planes)], pe.at[0 if ds < 0 else 1]
         else:
-            src, dst = (ed if ds > 0 else eu), pe.at[(df + 1) * 2 + (ds > 0)]
+            src = edge.at[pl.ds(planes + 1 if df > 0 else 0, 1)]
+            dst = pc.at[(df > 0) * 2 + (ds > 0)]
         return remote(src, dst, s_part.at[i], r_part.at[i], df, ds)
 
-    def gb_copy(ds):
-        j = 0 if ds > 0 else 1
-        r0, r1, rn = span(ds, HALO, rows, HALO, tall)
-        return remote(gbh.at[:, pl.ds(HALO + r1, rn), :], gbh.at[:, pl.ds(r0, rn), :],
-                      s_gb.at[j], r_gb.at[j], 0, ds)
-
-    for i, (df, ds) in enumerate(DIRS):
-        @pl.when(valid(df, ds))
-        def _(i=i, df=df, ds=ds):
-            sky_copy(i, df, ds).start()
-            if ds == 0:
-                hw_copy(df).start()
+    own.wait()
+    for ds in (-1, 1):
+        @pl.when(valid(0, ds))
+        def _(ds=ds):
+            for f in order:
+                sky_copy(ds, f).start()
 
     def cot_half(g, h):
         return cotv[g, :, h * HALF:(h + 1) * HALF, :].reshape(wide, length)
@@ -194,8 +195,9 @@
             if h < halves - 1:
                 total = total + jnp.where(r == HALF - 1, piece[h + 1][HALF + 1:HALF + 2], 0.0)
             part[p, h * HALF:(h + 1) * HALF] = total
-        ed[p:p + 1, :] = piece[-1][HALF:HALF + 1]
-        eu[p:p + 1, :] = piece[0][HALF + 1:HALF + 2]
+        for ref, line in ((ed, piece[-1][HALF:HALF + 1]), (eu, piece[0][HALF + 1:HALF + 2])):
+            n = length // 8
+            ref[p] = jnp.concatenate([line[:, j * n:(j + 1) * n] for j in range(8)], axis=0)
 
     for g in range(planes):
         cot_copies[g].wait()
@@ -210,17 +212,10 @@
         close_plane(g)
     close_plane(planes)
     close_plane(planes + 1)
-    eu[planes + 2:, :] = jnp.zeros((8 - planes - 2, length), F32)
-    ed[planes + 2:, :] = jnp.zeros((8 - planes - 2, length), F32)
     for i, (df, ds) in enumerate(DIRS):
         @pl.when(valid(df, ds))
         def _(i=i, df=df, ds=ds):
             part_copy(i, df, ds).start()
-
-    for df in (-1, 1):
-        @pl.when(valid(-df, 0))
-        def _(df=df):
-            hw_copy(df).wait_recv()
 
     def make_taps(p):
         h = hwb[p]
@@ -247,7 +242,7 @@
         hi = val.astype(BF16).astype(F32)
         trow[p] = jnp.where(lane < 2 * tall, hi, val - hi).astype(BF16)
 
-    for p in range(planes + 2):
+    for p in range(planes):
         make_taps(p)
 
     def blur(src, p, t):
@@ -263,50 +258,71 @@
         return jnp.dot(trow[t][:, :3 * tall], jnp.concatenate([hi, lo, hi], axis=0),
                        preferred_element_type=F32)
 
-    own.wait()
     for i, (df, ds) in enumerate(DIRS):
         @pl.when(valid(-df, -ds))
         def _(i=i, df=df, ds=ds):
-            sky_copy(i, df, ds).wait_recv()
-
-    for p in range(planes + 2):
-        beam = blur(skyh, p, p)
-        r = iota(beam.shape, 0)
-        outside = jnp.logical_or(jnp.logical_and(r == high - EDGE + HALF, si == ns - 1),
-                                 jnp.logical_and(r == HALF + 1, si == 0))
-        beam = jnp.where(outside, 0.0, beam)
+            part_copy(i, df, ds).wait_recv()
+    r = iota((rows, length), 0)
+    for f in order:
+        total = part[f + 1]
+        if f == 0:
+            total = total + pf[0]
+        if f == planes - 1:
+            total = total + pf[1]
+        for up in (0, 1):
+            line = pe[up, f]
+            if f == 0:
+                line = line + pc[2 + up, 0]
+            if f == planes - 1:
+                line = line + pc[up, 0]
+            line = jnp.concatenate([line[k:k + 1] for k in range(8)], axis=1)
+            total = total + jnp.where(r == (0 if up else rows - 1), line, 0.0)
+        gbh[f, HALO:HALO + rows, PAD:PAD + length] = total.astype(BF16)
+    for ds in (-1, 1):
+        @pl.when(valid(0, ds))
+        def _(ds=ds):
+            for f in order:
+                gb_copy(ds, f).start()
+
+    def spread_beam(p, beam):
         shifts = (shift_prev(beam), beam, shift_next(beam))
         for h in range(halves):
             bs[h, p] = jnp.concatenate(
                 [x[h * EDGE:(h + 1) * EDGE] for x in shifts] + [jnp.zeros((8, length), F32)],
                 axis=0).astype(BF16)
 
-    for i, (df, ds) in enumerate(DIRS):
-        @pl.when(valid(-df, -ds))
-        def _(i=i, df=df, ds=ds):
-            part_copy(i, df, ds).wait_recv()
-    r = iota((rows, length), 0)
-    for f in range(planes):
-        total = part[f + 1, 0:rows]
-        if f == 0:
-            total = total + pf[0]
-        if f == planes - 1:
-            total = total + pf[1]
-        for up in (0, 1):
-            line = pe[2 + up, f + 1:f + 2]
-            if f == 0:
-                line = line + pe[4 + up, planes + 1:planes + 2]
-            if f == planes - 1:
-                line = line + pe[up, 0:1]
-            total = total + jnp.where(r == (0 if up else rows - 1), line, 0.0)
-        gbh[f, HALO:HALO + rows, PAD:PAD + length] = total.astype(BF16)
-    for ds in (-1, 1):
-        @pl.when(valid(0, ds))
-        def _(ds=ds):
-            gb_copy(ds).start()
+    def wait_halo(make, f):
+        for ds in (-1, 1):
+            @pl.when(valid(0, -ds))
+            def _(ds=ds):
+                make(ds, f).wait_recv()
+
+    for f in order:
+        wait_halo(sky_copy, f)
+        beam = blur(skyh, f, f)
+        r = iota(beam.shape, 0)
+        outside = jnp.logical_or(jnp.logical_and(r == high - EDGE + HALF, si == ns - 1),
+                                 jnp.logical_and(r == HALF + 1, si == 0))
+        beam = jnp.where(outside, 0.0, beam)
+        if f in (0, planes - 1):
+            bm[f + 1] = beam.astype(BF16)
+            for df in (-1, 1):
+                if f == (planes - 1 if df > 0 else 0):
+                    @pl.when(valid(df, 0))
+                    def _(df=df):
+                        bm_copy(df).start()
+        spread_beam(f + 1, beam)
 
     acc2 = jnp.zeros((3 * TALL3, wide), F32)
-    for g in range(planes):
+    for g in list(range(1, planes - 1)) + [0, planes - 1]:
+        if g in (0, planes - 1):
+            df = 1 if g == 0 else -1
+
+            @pl.when(valid(-df, 0))
+            def _(df=df):
+                bm_copy(df).wait_recv()
+            p = 0 if g == 0 else planes + 1
+            spread_beam(p, bm[p].astype(F32))
         for h in range(halves):
             acc2 = acc2 + lax.dot_general(
                 bs[h, g:g + 3].reshape(3 * TALL3, length), cot_half(g, h),
@@ -342,21 +358,17 @@
     for k in range(1, ns):
         kg_copy(k, *over_sky).start()
 
-    for ds in (-1, 1):
-        @pl.when(valid(0, -ds))
-        def _(ds=ds):
-            gb_copy(ds).wait_recv()
-
     out_copies = [pltpu.make_async_copy(outv.at[f], out_ref.at[f], out_sem.at[f])
                   for f in range(planes)]
 
     def finish(f):
-        both = blur(gbh, f, f + 1)
+        wait_halo(gb_copy, f)
+        both = blur(gbh, f, f)
         for h in range(halves):
             outv[f, h * HALF:(h + 1) * HALF] = both[h * EDGE:h * EDGE + HALF]
         out_copies[f].start()
 
-    for f in range(planes // 2):
+    for f in order[:planes // 2]:
         finish(f)
     for k in range(1, ns):
         kg_wait(k, *over_sky)
@@ -367,7 +379,7 @@
     slots2[fi] = total
     for k in range(1, nf):
         kg_copy(k, *over_freq).start()
-    for f in range(planes // 2, planes):
+    for f in order[planes // 2:]:
         finish(f)
     for k in range(1, nf):
         kg_wait(k, *over_freq)
@@ -381,29 +393,28 @@
     for i, (df, ds) in enumerate(DIRS):
         @pl.when(valid(df, ds))
         def _(i=i, df=df, ds=ds):
-            sky_copy(i, df, ds).wait_send()
             part_copy(i, df, ds).wait_send()
             if ds == 0:
-                hw_copy(df).wait_send()
+                bm_copy(df).wait_send()
             if df == 0:
-                gb_copy(ds).wait_send()
+                for f in range(planes):
+                    sky_copy(ds, f).wait_send()
+                    gb_copy(ds, f).wait_send()
     for k in range(1, ns):
         kg_copy(k, *over_sky).wait_send()
     for k in range(1, nf):
         kg_copy(k, *over_freq).wait_send()
 
 
-def hand_on(sky_ref, packed_ref, out_ref, kg_ref, sems):
-    copies = [pltpu.make_async_copy(sky_ref.at[f], out_ref.at[f], sems.at[f])
-              for f in range(sky_ref.shape[0])]
-    for copy in copies:
-        copy.start()
-    packed = packed_ref[...]
-    half = packed.shape[0]
-    kg_ref[0:half] = packed[:, :27]
-    kg_ref[half:] = pltpu.roll(packed, 64, 1)[:, :27]
-    for copy in copies:
-        copy.wait()
+def hand_on(sky_ref, packed_ref, out_ref, kg_ref):
+    out_ref[...] = sky_ref[...]
+
+    @pl.when(pl.program_id(0) == 0)
+    def _():
+        packed = packed_ref[...]
+        half = packed.shape[0]
+        kg_ref[0:half] = packed[:, :27]
+        kg_ref[half:] = pltpu.roll(packed, 64, 1)[:, :27]
 
 
 def per_device(sky_cube, half_width, conv_weight, out_cotangent):
@@ -430,26 +441,29 @@
             pltpu.VMEM((planes, rows, length), F32), dma((planes,)),
             pltpu.SMEM((planes,), jnp.int32),
             pltpu.VMEM((chans, 27), BF16),
-            pltpu.VMEM((planes + 2, tall, length + 2 * PAD), BF16),
+            pltpu.VMEM((planes, tall, length + 2 * PAD), BF16),
             pltpu.VMEM((planes, tall, length + 2 * PAD), BF16),
             pltpu.VMEM((planes, chans, rows, length), BF16),
             pltpu.VMEM((9 * EDGE + 8, wide), BF16),
             pltpu.VMEM((planes + 2, halves, 3, EDGE, length), F32),
             pltpu.VMEM((planes + 2, rows, length), F32),
-            pltpu.VMEM((8, length), F32),
-            pltpu.VMEM((8, length), F32),
+            pltpu.VMEM((planes + 2, 8, length // 8), F32),
+            pltpu.VMEM((planes + 2, 8, length // 8), F32),
             pltpu.VMEM((2, rows, length), F32),
-            pltpu.VMEM((6, 8, length), F32),
+            pltpu.VMEM((2, planes, 8, length // 8), F32),
+            pltpu.VMEM((4, 1, 8, length // 8), F32),
+            pltpu.VMEM((planes + 2, high, length), BF16),
             pltpu.VMEM((halves, planes + 2, TALL3, length), BF16),
-            pltpu.VMEM((planes + 2, 3 * BLOCK, 2 * BLOCK), BF16),
-            pltpu.VMEM((planes + 2, high, 256), BF16),
-            pltpu.VMEM((planes + 2, 8, 256), F32),
+            pltpu.VMEM((planes, 3 * BLOCK, 2 * BLOCK), BF16),
+            pltpu.VMEM((planes, high, 256), BF16),
+            pltpu.VMEM((planes, 8, 256), F32),
             pltpu.VMEM((chans // 2, 128), F32),
             pltpu.VMEM((ns, chans // 2, 128), F32),
             pltpu.VMEM((chans // 2, 128), F32),
             pltpu.VMEM((nf, chans // 2, 128), F32),
             dma((planes,)), dma((3,)),
-            dma((8,)), dma((8,)), dma((2,)), dma((2,)), dma((8,)), dma((8,)), dma((2,)), dma((2,)),
+            dma((2 * planes,)), dma((2 * planes,)), dma((8,)), dma((8,)),
+            dma((2 * planes,)), dma((2 * planes,)), dma((2,)), dma((2,)),
             dma((ns,)), dma((ns,)), dma((nf,)), dma((nf,)),
         ],
         compiler_params=pltpu.CompilerParams(
@@ -460,9 +474,11 @@
         hand_on,
         out_shape=(jax.ShapeDtypeStruct((planes, rows, length), F32),
                    jax.ShapeDtypeStruct((chans, 27), F32)),
-        in_specs=[pl.BlockSpec(memory_space=pltpu.HBM), pl.BlockSpec(memory_space=pltpu.VMEM)],
-        out_specs=(pl.BlockSpec(memory_space=pltpu.HBM), pl.BlockSpec(memory_space=pltpu.VMEM)),
-        scratch_shapes=[dma((planes,))],
+        grid=(2,),
+        in_specs=[pl.BlockSpec((planes // 2, rows, length), lambda f: (f, 0, 0)),
+                  pl.BlockSpec((chans // 2, 128), lambda f: (0, 0))],
+        out_specs=(pl.BlockSpec((planes // 2, rows, length), lambda f: (f, 0, 0)),
+                   pl.BlockSpec((chans, 27), lambda f: (0, 0))),
         compiler_params=pltpu.CompilerParams(vmem_limit_bytes=60 * 1024 * 1024),
         name="hand_on",
     )(sky_grad, packed)

time: 51.6 us -> 30.1 us (0.58)
  the two profiles are of different devices: /device:TPU:9 before, /device:TPU:0 now
where the time goes in v3:
time: 30.1 us; the launch traced here: 29.9 us
  Pallas kernels  29.3 us (97%)
  between operations  0.64 us (2%)
    pallas_call x1, Pallas kernels, per_device(): pl.pallas_call(kernel, out_shape=(jax.ShapeDtypeStruct((planes, rows, len...  27.5 us
    pallas_call x1, Pallas kernels, per_device(): pl.pallas_call(hand_on, out_shape=(jax.ShapeDtypeStruct((planes, rows, le...  1.84 us

profile of v3, /device:TPU:0, one launch (start us, length us, event | category | flops | bytes accessed | tf_op | source)
XLA Modules:
  0.0 29.9 jit_solution(15520706158851495871)
XLA Ops:
  0.6 27.5 %beam_backward.1 = (f32[4,32,1024]{2,1,0:T(8,128)}, f32[8,128]{1,0:T(8,128)}) custom-call(s32[4]{0:T(128)} %refs_0_.1, bf16[4,32,1024]{2,1,0:T(8,128)(2,1)} %refs_1_.1, bf16[16,27]{1,0:T(8,128)(2,1)} %refs_2_.1, bf16[16,4,32,1024]{3,2,1,0:T(8,128)(2,1)} %refs_3_.1), custom_call_target="tpu_custom_call" | custom-call | tf_op jit(solution)/shard_map/beam_backward/pallas_call | solution.py:434
  28.1 1.8 %hand_on.1 = (f32[4,32,1024]{2,1,0:T(8,128)}, f32[16,27]{1,0:T(8,128)}) custom-call(f32[4,32,1024]{2,1,0:T(8,128)} %get-tuple-element.4.sky_ref, f32[8,128]{1,0:T(8,128)} %get-tuple-element.5.packed_ref), custom_call_target="tpu_custom_call" | custom-call | tf_op jit(solution)/shard_map/hand_on/pallas_call | solution.py:473

commit v4 on v3

--- a/solution.py
+++ b/solution.py
@@ -73,6 +73,7 @@
 
     lanes = pl.ds(PAD, length)
     order = [0, planes - 1] + list(range(1, planes - 1))
+    pairs = [order[k:k + 2] for k in range(0, planes, 2)]
 
     own_w = pltpu.make_async_copy(w_hbm, w_ref, own_sem.at[1])
     own_w.start()
@@ -219,44 +220,85 @@
 
     def make_taps(p):
         h = hwb[p]
-        h2 = h * h
-
-        def profile(d, reach, reach2):
+        fall = -2.0 / (h * h)
+
+        def profile(d, reach, fall):
             d = d.astype(F32)
-            return jnp.where(jnp.abs(d) <= reach, jnp.exp(-2.0 * (d * d) / reach2), 0.0)
+            return jnp.where(jnp.abs(d) <= reach, jnp.exp((d * d) * fall), 0.0)
 
         lane = iota((8, 256), 1)
-        small = jnp.where(lane <= 2 * MAXH, profile(lane - MAXH, h, h2), 0.0)
+        small = jnp.where(lane <= 2 * MAXH, profile(lane - MAXH, h, fall), 0.0)
         inv = 1.0 / jnp.sqrt(jnp.sum(small * small, axis=1, keepdims=True))
         inv = jnp.broadcast_to(inv, (8, 256))[0:1]
-        h, h2 = h[0:1], h2[0:1]
+        h, fall = h[0:1], fall[0:1]
         shape = (3 * BLOCK, BLOCK)
-        val = profile(iota(shape, 0) - BLOCK - iota(shape, 1), h[:, :BLOCK], h2[:, :BLOCK]) * inv[:, :BLOCK]
+        val = profile(iota(shape, 0) - BLOCK - iota(shape, 1), h[:, :BLOCK], fall[:, :BLOCK]) * inv[:, :BLOCK]
         hi = val.astype(BF16)
         tcol[p, :, 0:BLOCK] = hi
         tcol[p, :, BLOCK:] = (val - hi.astype(F32)).astype(BF16)
-        shape = (high, 256)
+        shape = (high, 4 * tall)
         lane = iota(shape, 1)
         row = row_of(lax.rem(iota(shape, 0), EDGE), HALF) + HALF * lax.div(iota(shape, 0), EDGE)
-        val = profile(lax.rem(lane, tall) - HALO - row, h, h2) * inv
+        val = profile(lax.rem(lane, tall) - HALO - row, h, fall) * inv
         hi = val.astype(BF16).astype(F32)
-        trow[p] = jnp.where(lane < 2 * tall, hi, val - hi).astype(BF16)
+        at = lane - 2 * tall * (order.index(p) % 2)
+        here = jnp.logical_and(at >= 0, at < 2 * tall)
+        first = jnp.logical_and(at >= 0, at < tall)
+        trow[p, 0:high] = jnp.where(here, hi, 0.0).astype(BF16)
+        trow[p, high:] = jnp.where(first, val - hi, 0.0).astype(BF16)
 
     for p in range(planes):
         make_taps(p)
 
-    def blur(src, p, t):
+    def blur(src, pair):
         blocks = length // BLOCK
-        field = jnp.concatenate(
-            [src[p, :, j * BLOCK:(j + 3) * BLOCK] for j in range(blocks)], axis=0)
-        both = jnp.dot(field, tcol[t], preferred_element_type=F32)
-        q = both[:, :BLOCK] + both[:, BLOCK:]
-        hi = q.astype(BF16)
-        lo = (q - hi.astype(F32)).astype(BF16)
-        hi = jnp.concatenate([hi[j * tall:(j + 1) * tall] for j in range(blocks)], axis=1)
-        lo = jnp.concatenate([lo[j * tall:(j + 1) * tall] for j in range(blocks)], axis=1)
-        return jnp.dot(trow[t][:, :3 * tall], jnp.concatenate([hi, lo, hi], axis=0),
-                       preferred_element_type=F32)
+        parts = []
+        for p in pair:
+            field = jnp.concatenate(
+                [src[p, :, j * BLOCK:(j + 3) * BLOCK] for j in range(blocks)], axis=0)
+            both = jnp.dot(field, tcol[p], preferred_element_type=F32)
+            q = both[:, :BLOCK] + both[:, BLOCK:]
+            hi = q.astype(BF16)
+            lo = (q - hi.astype(F32)).astype(BF16)
+            for x in (hi, lo):
+                parts.append(jnp.concatenate(
+                    [x[j * tall:(j + 1) * tall] for j in range(blocks)], axis=1))
+        left = jnp.concatenate([trow[p] for p in pair], axis=0)
+        res = jnp.dot(left, jnp.concatenate(parts, axis=0), preferred_element_type=F32)
+        return [res[2 * i * high:(2 * i + 1) * high] + res[(2 * i + 1) * high:(2 * i + 2) * high]
+                for i in range(len(pair))]
+
+    def spread_beam(p, beam):
+        shifts = (shift_prev(beam), beam, shift_next(beam))
+        for h in range(halves):
+            bs[h, p] = jnp.concatenate(
+                [x[h * EDGE:(h + 1) * EDGE] for x in shifts] + [jnp.zeros((8, length), F32)],
+                axis=0).astype(BF16)
+
+    def wait_halos(make, which):
+        for ds in (-1, 1):
+            @pl.when(valid(0, -ds))
+            def _(ds=ds):
+                for f in which:
+                    make(ds, f).wait_recv()
+
+    def make_beams(pair):
+        beams = blur(skyh, pair)
+        r = iota(beams[0].shape, 0)
+        outside = jnp.logical_or(jnp.logical_and(r == high - EDGE + HALF, si == ns - 1),
+                                 jnp.logical_and(r == HALF + 1, si == 0))
+        for f, beam in zip(pair, beams):
+            beam = jnp.where(outside, 0.0, beam)
+            if f in (0, planes - 1):
+                bm[f + 1] = beam.astype(BF16)
+            spread_beam(f + 1, beam)
+
+    wait_halos(sky_copy, order)
+    make_beams(pairs[0])
+    for df in (-1, 1):
+        @pl.when(valid(df, 0))
+        def _(df=df):
+            bm_copy(df).start()
 
     for i, (df, ds) in enumerate(DIRS):
         @pl.when(valid(-df, -ds))
@@ -284,49 +326,27 @@
             for f in order:
                 gb_copy(ds, f).start()
 
-    def spread_beam(p, beam):
-        shifts = (shift_prev(beam), beam, shift_next(beam))
+    for pair in pairs[1:]:
+        make_beams(pair)
+
+    acc2 = jnp.zeros((3 * TALL3, wide), F32)
+    def gram(total, g):
         for h in range(halves):
-            bs[h, p] = jnp.concatenate(
-                [x[h * EDGE:(h + 1) * EDGE] for x in shifts] + [jnp.zeros((8, length), F32)],
-                axis=0).astype(BF16)
-
-    def wait_halo(make, f):
-        for ds in (-1, 1):
-            @pl.when(valid(0, -ds))
-            def _(ds=ds):
-                make(ds, f).wait_recv()
-
-    for f in order:
-        wait_halo(sky_copy, f)
-        beam = blur(skyh, f, f)
-        r = iota(beam.shape, 0)
-        outside = jnp.logical_or(jnp.logical_and(r == high - EDGE + HALF, si == ns - 1),
-                                 jnp.logical_and(r == HALF + 1, si == 0))
-        beam = jnp.where(outside, 0.0, beam)
-        if f in (0, planes - 1):
-            bm[f + 1] = beam.astype(BF16)
-            for df in (-1, 1):
-                if f == (planes - 1 if df > 0 else 0):
-                    @pl.when(valid(df, 0))
-                    def _(df=df):
-                        bm_copy(df).start()
-        spread_beam(f + 1, beam)
-
-    acc2 = jnp.zeros((3 * TALL3, wide), F32)
-    for g in list(range(1, planes - 1)) + [0, planes - 1]:
-        if g in (0, planes - 1):
-            df = 1 if g == 0 else -1
-
-            @pl.when(valid(-df, 0))
-            def _(df=df):
-                bm_copy(df).wait_recv()
-            p = 0 if g == 0 else planes + 1
-            spread_beam(p, bm[p].astype(F32))
-        for h in range(halves):
-            acc2 = acc2 + lax.dot_general(
+            total = total + lax.dot_general(
                 bs[h, g:g + 3].reshape(3 * TALL3, length), cot_half(g, h),
                 (((1,), (1,)), ((), ())), preferred_element_type=F32)
+        return total
+
+    for g in range(1, planes - 1):
+        acc2 = gram(acc2, g)
+    for df in (-1, 1):
+        @pl.when(valid(-df, 0))
+        def _(df=df):
+            bm_copy(df).wait_recv()
+    for p in (0, planes + 1):
+        spread_beam(p, bm[p].astype(F32))
+    for g in (0, planes - 1):
+        acc2 = gram(acc2, g)
     lines = []
     for a in range(3):
         for b in range(3):
@@ -361,15 +381,14 @@
     out_copies = [pltpu.make_async_copy(outv.at[f], out_ref.at[f], out_sem.at[f])
                   for f in range(planes)]
 
-    def finish(f):
-        wait_halo(gb_copy, f)
-        both = blur(gbh, f, f)
-        for h in range(halves):
-            outv[f, h * HALF:(h + 1) * HALF] = both[h * EDGE:h * EDGE + HALF]
-        out_copies[f].start()
-
-    for f in order[:planes // 2]:
-        finish(f)
+    def finish(pair):
+        for f, both in zip(pair, blur(gbh, pair)):
+            for h in range(halves):
+                outv[f, h * HALF:(h + 1) * HALF] = both[h * EDGE:h * EDGE + HALF]
+            out_copies[f].start()
+
+    wait_halos(gb_copy, order)
+    finish(pairs[0])
     for k in range(1, ns):
         kg_wait(k, *over_sky)
     total = slots[0]
@@ -379,8 +398,8 @@
     slots2[fi] = total
     for k in range(1, nf):
         kg_copy(k, *over_freq).start()
-    for f in order[planes // 2:]:
-        finish(f)
+    for pair in pairs[1:]:
+        finish(pair)
     for k in range(1, nf):
         kg_wait(k, *over_freq)
     total = slots2[0]
@@ -455,7 +474,7 @@
             pltpu.VMEM((planes + 2, high, length), BF16),
             pltpu.VMEM((halves, planes + 2, TALL3, length), BF16),
             pltpu.VMEM((planes, 3 * BLOCK, 2 * BLOCK), BF16),
-            pltpu.VMEM((planes, high, 256), BF16),
+            pltpu.VMEM((planes, 2 * high, 4 * tall), BF16),
             pltpu.VMEM((planes, 8, 256), F32),
             pltpu.VMEM((chans // 2, 128), F32),
             pltpu.VMEM((ns, chans // 2, 128), F32),

time: 30.1 us -> 28.9 us (0.960)
  Pallas kernels: 29.3 us -> 28.2 us
    pallas_call x1, Pallas kernels: 27.5 us -> 26.3 us  [per_device(): pl.pallas_call(kernel, out_shape=(jax.ShapeDtypeStruct((planes, rows, len...]
where the time goes in v4:
time: 28.9 us; the launch traced here: 28.8 us
  Pallas kernels  28.2 us (98%)
  between operations  0.64 us (2%)
    pallas_call x1, Pallas kernels, per_device(): pl.pallas_call(kernel, out_shape=(jax.ShapeDtypeStruct((planes, rows, len...  26.3 us
    pallas_call x1, Pallas kernels, per_device(): pl.pallas_call(hand_on, out_shape=(jax.ShapeDtypeStruct((planes, rows, le...  1.84 us

profile of v4, /device:TPU:0, one launch (start us, length us, event | category | flops | bytes accessed | tf_op | source)
XLA Modules:
  0.0 28.8 jit_solution(2458425658866875886)
XLA Ops:
  0.6 26.3 %beam_backward.1 = (f32[4,32,1024]{2,1,0:T(8,128)}, f32[8,128]{1,0:T(8,128)}) custom-call(s32[4]{0:T(128)} %refs_0_.1, bf16[4,32,1024]{2,1,0:T(8,128)(2,1)} %refs_1_.1, bf16[16,27]{1,0:T(8,128)(2,1)} %refs_2_.1, bf16[16,4,32,1024]{3,2,1,0:T(8,128)(2,1)} %refs_3_.1), custom_call_target="tpu_custom_call" | custom-call | tf_op jit(solution)/shard_map/beam_backward/pallas_call | solution.py:453
  26.9 1.8 %hand_on.1 = (f32[4,32,1024]{2,1,0:T(8,128)}, f32[16,27]{1,0:T(8,128)}) custom-call(f32[4,32,1024]{2,1,0:T(8,128)} %get-tuple-element.4.sky_ref, f32[8,128]{1,0:T(8,128)} %get-tuple-element.5.packed_ref), custom_call_target="tpu_custom_call" | custom-call | tf_op jit(solution)/shard_map/hand_on/pallas_call | solution.py:492

commit v5 on v4

--- a/solution.py
+++ b/solution.py
@@ -44,7 +44,7 @@
 
 
 def body(nf, ns, scale, hw_hbm, sky_ref, w_hbm, cot_ref, out_ref, kg_ref,
-         outv, out_sem, hw_ref, w_ref, skyh, gbh, cotv, bmat, acc, part, eu, ed, pf, pe, pc,
+         outv, out_sem, hw_ref, w_ref, skyh, gbh, gs, cotv, bmat, acc, part, eu, ed, pf, pe, pc,
          bm, bs, tcol, trow, hwb, mine, slots, mine2, slots2,
          cot_sem, own_sem, s_sky, r_sky, s_part, r_part, s_gb, r_gb, s_bm, r_bm,
          s_kg, r_kg, s_kf, r_kf):
@@ -157,7 +157,32 @@
         return halo_copy(skyh, s_sky, r_sky, ds, f)
 
     def gb_copy(ds, f):
-        return halo_copy(gbh, s_gb, r_gb, ds, f)
+        i = (ds > 0) * planes + f
+        r0, _, rn = span(ds, HALO, rows, HALO, tall)
+        return remote(gs.at[(ds > 0) * 1, f], gbh.at[f, pl.ds(r0, rn), lanes],
+                      s_gb.at[i], r_gb.at[i], 0, ds)
+
+    spare = HALO - MAXH
+    guest = planes - 1
+    assert spare * guest == MAXH
+    tile_row = iota((HALO, length), 0)
+
+    def pack_halo(ds, f, own_tile, guest_tile):
+        if ds > 0:
+            return jnp.where(tile_row < spare,
+                             pltpu.roll(guest_tile, HALO - spare * (f + 1), 0), own_tile)
+        return jnp.where(tile_row >= MAXH, pltpu.roll(guest_tile, MAXH - spare * f, 0), own_tile)
+
+    def unpack_guest(ds):
+        r0, _, rn = span(ds, HALO, rows, HALO, tall)
+        tile = jnp.zeros((HALO, length), F32)
+        for f in range(guest):
+            got = gbh[f, r0:r0 + rn, PAD:PAD + length].astype(F32)
+            first = spare * (f + 1) if ds > 0 else spare * f
+            shift = first if ds > 0 else (first + HALO - MAXH) % HALO
+            here = jnp.logical_and(tile_row >= first, tile_row < first + spare)
+            tile = jnp.where(here, pltpu.roll(got, shift, 0) if shift else got, tile)
+        gbh[guest, r0:r0 + rn, PAD:PAD + length] = tile.astype(BF16)
 
     def bm_copy(df):
         j = 0 if df > 0 else 1
@@ -305,6 +330,7 @@
         def _(i=i, df=df, ds=ds):
             part_copy(i, df, ds).wait_recv()
     r = iota((rows, length), 0)
+    sums = {}
     for f in order:
         total = part[f + 1]
         if f == 0:
@@ -319,11 +345,16 @@
                 line = line + pc[up, 0]
             line = jnp.concatenate([line[k:k + 1] for k in range(8)], axis=1)
             total = total + jnp.where(r == (0 if up else rows - 1), line, 0.0)
+        sums[f] = total
         gbh[f, HALO:HALO + rows, PAD:PAD + length] = total.astype(BF16)
+    for f in range(guest):
+        gs[0, f] = pack_halo(-1, f, sums[f][:HALO], sums[guest][:HALO]).astype(BF16)
+        gs[1, f] = pack_halo(1, f, sums[f][rows - HALO:], sums[guest][rows - HALO:]).astype(BF16)
+    gb_order = pairs[1] + pairs[0][:1]
     for ds in (-1, 1):
         @pl.when(valid(0, ds))
         def _(ds=ds):
-            for f in order:
+            for f in gb_order:
                 gb_copy(ds, f).start()
 
     for pair in pairs[1:]:
@@ -387,8 +418,8 @@
                 outv[f, h * HALF:(h + 1) * HALF] = both[h * EDGE:h * EDGE + HALF]
             out_copies[f].start()
 
-    wait_halos(gb_copy, order)
-    finish(pairs[0])
+    wait_halos(gb_copy, pairs[1])
+    finish(pairs[1])
     for k in range(1, ns):
         kg_wait(k, *over_sky)
     total = slots[0]
@@ -398,8 +429,10 @@
     slots2[fi] = total
     for k in range(1, nf):
         kg_copy(k, *over_freq).start()
-    for pair in pairs[1:]:
-        finish(pair)
+    wait_halos(gb_copy, pairs[0][:1])
+    for ds in (-1, 1):
+        unpack_guest(ds)
+    finish(pairs[0])
     for k in range(1, nf):
         kg_wait(k, *over_freq)
     total = slots2[0]
@@ -418,7 +451,8 @@
             if df == 0:
                 for f in range(planes):
                     sky_copy(ds, f).wait_send()
-                    gb_copy(ds, f).wait_send()
+                    if f != guest:
+                        gb_copy(ds, f).wait_send()
     for k in range(1, ns):
         kg_copy(k, *over_sky).wait_send()
     for k in range(1, nf):
@@ -462,6 +496,7 @@
             pltpu.VMEM((chans, 27), BF16),
             pltpu.VMEM((planes, tall, length + 2 * PAD), BF16),
             pltpu.VMEM((planes, tall, length + 2 * PAD), BF16),
+            pltpu.VMEM((2, planes - 1, HALO, length), BF16),
             pltpu.VMEM((planes, chans, rows, length), BF16),
             pltpu.VMEM((9 * EDGE + 8, wide), BF16),
             pltpu.VMEM((planes + 2, halves, 3, EDGE, length), F32),

time: 28.9 us -> 28.9 us (level)
  no operation moved by 1% of the time
where the time goes in v5:
time: 28.9 us; the launch traced here: 28.8 us
  Pallas kernels  28.1 us (97%)
  between operations  0.64 us (2%)
    pallas_call x1, Pallas kernels, per_device(): pl.pallas_call(kernel, out_shape=(jax.ShapeDtypeStruct((planes, rows, len...  26.3 us
    pallas_call x1, Pallas kernels, per_device(): pl.pallas_call(hand_on, out_shape=(jax.ShapeDtypeStruct((planes, rows, le...  1.84 us

profile of v5, /device:TPU:0, one launch (start us, length us, event | category | flops | bytes accessed | tf_op | source)
XLA Modules:
  0.0 28.8 jit_solution(6251641100788908573)
XLA Ops:
  0.6 26.3 %beam_backward.1 = (f32[4,32,1024]{2,1,0:T(8,128)}, f32[8,128]{1,0:T(8,128)}) custom-call(s32[4]{0:T(128)} %refs_0_.1, bf16[4,32,1024]{2,1,0:T(8,128)(2,1)} %refs_1_.1, bf16[16,27]{1,0:T(8,128)(2,1)} %refs_2_.1, bf16[16,4,32,1024]{3,2,1,0:T(8,128)(2,1)} %refs_3_.1), custom_call_target="tpu_custom_call" | custom-call | tf_op jit(solution)/shard_map/beam_backward/pallas_call | solution.py:487
  26.9 1.8 %hand_on.1 = (f32[4,32,1024]{2,1,0:T(8,128)}, f32[16,27]{1,0:T(8,128)}) custom-call(f32[4,32,1024]{2,1,0:T(8,128)} %get-tuple-element.4.sky_ref, f32[8,128]{1,0:T(8,128)} %get-tuple-element.5.packed_ref), custom_call_target="tpu_custom_call" | custom-call | tf_op jit(solution)/shard_map/hand_on/pallas_call | solution.py:527

commit v6 on v4

--- a/solution.py
+++ b/solution.py
@@ -425,15 +425,21 @@
         kg_copy(k, *over_freq).wait_send()
 
 
-def hand_on(sky_ref, packed_ref, out_ref, kg_ref):
-    out_ref[...] = sky_ref[...]
-
-    @pl.when(pl.program_id(0) == 0)
-    def _():
-        packed = packed_ref[...]
-        half = packed.shape[0]
-        kg_ref[0:half] = packed[:, :27]
-        kg_ref[half:] = pltpu.roll(packed, 64, 1)[:, :27]
+def hand_on(sky_ref, packed_ref, out_ref, kg_ref, held, in_sem, out_sem):
+    planes = sky_ref.shape[0]
+    arrive = [pltpu.make_async_copy(sky_ref.at[f], held.at[f], in_sem.at[f]) for f in range(planes)]
+    leave = [pltpu.make_async_copy(held.at[f], out_ref.at[f], out_sem.at[f]) for f in range(planes)]
+    for copy in arrive:
+        copy.start()
+    for f in range(planes):
+        arrive[f].wait()
+        leave[f].start()
+    packed = packed_ref[...]
+    half = packed.shape[0]
+    kg_ref[0:half] = packed[:, :27]
+    kg_ref[half:] = pltpu.roll(packed, 64, 1)[:, :27]
+    for copy in leave:
+        copy.wait()
 
 
 def per_device(sky_cube, half_width, conv_weight, out_cotangent):
@@ -493,11 +499,9 @@
         hand_on,
         out_shape=(jax.ShapeDtypeStruct((planes, rows, length), F32),
                    jax.ShapeDtypeStruct((chans, 27), F32)),
-        grid=(2,),
-        in_specs=[pl.BlockSpec((planes // 2, rows, length), lambda f: (f, 0, 0)),
-                  pl.BlockSpec((chans // 2, 128), lambda f: (0, 0))],
-        out_specs=(pl.BlockSpec((planes // 2, rows, length), lambda f: (f, 0, 0)),
-                   pl.BlockSpec((chans, 27), lambda f: (0, 0))),
+        in_specs=[pl.BlockSpec(memory_space=pltpu.HBM), pl.BlockSpec(memory_space=pltpu.VMEM)],
+        out_specs=(pl.BlockSpec(memory_space=pltpu.HBM), pl.BlockSpec(memory_space=pltpu.VMEM)),
+        scratch_shapes=[pltpu.VMEM((planes, rows, length), F32), dma((planes,)), dma((planes,))],
         compiler_params=pltpu.CompilerParams(vmem_limit_bytes=60 * 1024 * 1024),
         name="hand_on",
     )(sky_grad, packed)

time: 28.9 us -> 30.2 us (1.045)
  Pallas kernels: 28.2 us -> 29.4 us
    pallas_call x1, Pallas kernels: 1.84 us -> 3.09 us  [per_device(): pl.pallas_call(hand_on, out_shape=(jax.ShapeDtypeStruct((planes, rows, le...]
where the time goes in v6:
time: 30.2 us; the launch traced here: 30 us
  Pallas kernels  29.4 us (97%)
  between operations  0.64 us (2%)
    pallas_call x1, Pallas kernels, per_device(): pl.pallas_call(kernel, out_shape=(jax.ShapeDtypeStruct((planes, rows, len...  26.3 us
    pallas_call x1, Pallas kernels, per_device(): pl.pallas_call(hand_on, out_shape=(jax.ShapeDtypeStruct((planes, rows, le...  3.09 us

profile of v6, /device:TPU:0, one launch (start us, length us, event | category | flops | bytes accessed | tf_op | source)
XLA Modules:
  0.0 30.0 jit_solution(4982208776028335313)
XLA Ops:
  0.6 26.3 %beam_backward.1 = (f32[4,32,1024]{2,1,0:T(8,128)}, f32[8,128]{1,0:T(8,128)}) custom-call(s32[4]{0:T(128)} %refs_0_.1, bf16[4,32,1024]{2,1,0:T(8,128)(2,1)} %refs_1_.1, bf16[16,27]{1,0:T(8,128)(2,1)} %refs_2_.1, bf16[16,4,32,1024]{3,2,1,0:T(8,128)(2,1)} %refs_3_.1), custom_call_target="tpu_custom_call" | custom-call | tf_op jit(solution)/shard_map/beam_backward/pallas_call | solution.py:459
  26.9 3.1 %hand_on.1 = (f32[4,32,1024]{2,1,0:T(8,128)}, f32[16,27]{1,0:T(8,128)}) custom-call(f32[4,32,1024]{2,1,0:T(8,128)} %get-tuple-element.4.sky_ref, f32[8,128]{1,0:T(8,128)} %get-tuple-element.5.packed_ref), custom_call_target="tpu_custom_call" | custom-call | tf_op jit(solution)/shard_map/hand_on/pallas_call | solution.py:498

commit v7 on v4

--- a/solution.py
+++ b/solution.py
@@ -493,10 +493,10 @@
         hand_on,
         out_shape=(jax.ShapeDtypeStruct((planes, rows, length), F32),
                    jax.ShapeDtypeStruct((chans, 27), F32)),
-        grid=(2,),
-        in_specs=[pl.BlockSpec((planes // 2, rows, length), lambda f: (f, 0, 0)),
+        grid=(planes,),
+        in_specs=[pl.BlockSpec((1, rows, length), lambda f: (f, 0, 0)),
                   pl.BlockSpec((chans // 2, 128), lambda f: (0, 0))],
-        out_specs=(pl.BlockSpec((planes // 2, rows, length), lambda f: (f, 0, 0)),
+        out_specs=(pl.BlockSpec((1, rows, length), lambda f: (f, 0, 0)),
                    pl.BlockSpec((chans, 27), lambda f: (0, 0))),
         compiler_params=pltpu.CompilerParams(vmem_limit_bytes=60 * 1024 * 1024),
         name="hand_on",

time: 28.9 us -> 30.4 us (1.052)
  Pallas kernels: 28.2 us -> 29.5 us
    pallas_call x1, Pallas kernels: 1.84 us -> 3.23 us  [per_device(): pl.pallas_call(hand_on, out_shape=(jax.ShapeDtypeStruct((planes, rows, le...]
where the time goes in v7:
time: 30.4 us; the launch traced here: 30.2 us
  Pallas kernels  29.5 us (97%)
  between operations  0.64 us (2%)
    pallas_call x1, Pallas kernels, per_device(): pl.pallas_call(kernel, out_shape=(jax.ShapeDtypeStruct((planes, rows, len...  26.3 us
    pallas_call x1, Pallas kernels, per_device(): pl.pallas_call(hand_on, out_shape=(jax.ShapeDtypeStruct((planes, rows, le...  3.23 us

profile of v7, /device:TPU:0, one launch (start us, length us, event | category | flops | bytes accessed | tf_op | source)
XLA Modules:
  0.0 30.2 jit_solution(18070897855823904967)
XLA Ops:
  0.6 26.3 %beam_backward.1 = (f32[4,32,1024]{2,1,0:T(8,128)}, f32[8,128]{1,0:T(8,128)}) custom-call(s32[4]{0:T(128)} %refs_0_.1, bf16[4,32,1024]{2,1,0:T(8,128)(2,1)} %refs_1_.1, bf16[16,27]{1,0:T(8,128)(2,1)} %refs_2_.1, bf16[16,4,32,1024]{3,2,1,0:T(8,128)(2,1)} %refs_3_.1), custom_call_target="tpu_custom_call" | custom-call | tf_op jit(solution)/shard_map/beam_backward/pallas_call | solution.py:453
  26.9 3.2 %hand_on.1 = (f32[4,32,1024]{2,1,0:T(8,128)}, f32[16,27]{1,0:T(8,128)}) custom-call(f32[4,32,1024]{2,1,0:T(8,128)} %get-tuple-element.4.sky_ref, f32[8,128]{1,0:T(8,128)} %get-tuple-element.5.packed_ref), custom_call_target="tpu_custom_call" | custom-call | tf_op jit(solution)/shard_map/hand_on/pallas_call | solution.py:492
